TPU v7x, 128 devices: a whole 4x4x4 slice. The times are simulated.
128 devices in a mesh: gz: 16 (over z, y), xy: 8 (over x, core).
Axes of the slice: x: 4, y: 4, z: 4, core: 2. Of those that a mesh axis runs over, the one named last changes fastest.
Arguments:
- volume: float32 [256, 256, 128], P('gz', 'xy'), may hold values from -6 to 6
- owners: int32 [8, 64, 1], P('xy', 'gz'), may hold values from 0 to 15; in each aligned block of 4 rows (0 to 3, 4 to 7, ..., all dimensions but the last counted through in order) at most 2 rows name the same one
Outputs:
- denoised: float32 [256, 256, 128], P('gz', 'xy')
- routed: float32 [8, 512, 128, 128], P('xy', 'gz')
Inputs may be any that keep to these rules, and one draw needn't show every extreme that they name: `owners`: among the 4 blocks of one device no destination is named more than 2 times, a bound that some block reaches.
All inputs are finite; a program needn't handle non-finite values.
Results may differ from a plain program's by a relative error of at most 0.0003.
Values sent between devices are 32-bit elements; how exact they have to be, the bound alone decides.
A program may use at most 64 MiB of HBM per device.

v0:
```python
import jax
import jax.numpy as jnp
from jax import lax
from jax.sharding import PartitionSpec as P

STEPS = 2
MOST = 2
BLOCK_ROWS = 128


TIME_STEP = 30.0
CONTRAST = 4.0


def with_halo(block, sides, width):
    for axis, dim in sides:
        count = lax.axis_size(axis)
        forward = [(i, i + 1) for i in range(count - 1)]
        backward = [(target, source) for source, target in forward]
        low = lax.ppermute(
            lax.slice_in_dim(block, block.shape[dim] - width, None, axis=dim), axis, forward
        )
        high = lax.ppermute(lax.slice_in_dim(block, 0, width, axis=dim), axis, backward)
        block = jnp.concatenate([low, block, high], axis=dim)
    return block


def shifted(field, stride, line_axis, fill, before):
    length = field.shape[line_axis]
    shape = list(field.shape)
    shape[line_axis] = stride
    padding = jnp.full(tuple(shape), fill, field.dtype)
    if before:
        return jnp.concatenate(
            [padding, lax.slice_in_dim(field, 0, length - stride, axis=line_axis)], axis=line_axis
        )
    return jnp.concatenate(
        [lax.slice_in_dim(field, stride, length, axis=line_axis), padding], axis=line_axis
    )


def cyclic_solve(low_diag, main_diag, high_diag, right_side, line_axis, side_axis):
    length = main_diag.shape[line_axis]
    stride = 1
    while stride < length:
        low_prev = shifted(low_diag, stride, line_axis, 0.0, True)
        main_prev = shifted(main_diag, stride, line_axis, 1.0, True)
        high_prev = shifted(high_diag, stride, line_axis, 0.0, True)
        side_prev = shifted(right_side, stride, side_axis, 0.0, True)
        low_next = shifted(low_diag, stride, line_axis, 0.0, False)
        main_next = shifted(main_diag, stride, line_axis, 1.0, False)
        high_next = shifted(high_diag, stride, line_axis, 0.0, False)
        side_next = shifted(right_side, stride, side_axis, 0.0, False)
        factor_low = -low_diag / main_prev
        factor_high = -high_diag / main_next
        main_diag = main_diag + factor_low * high_prev + factor_high * low_next
        right_side = right_side + factor_low * side_prev + factor_high * side_next
        low_diag = factor_low * low_prev
        high_diag = factor_high * high_next
        stride = stride * 2
    return right_side / main_diag


def coefficients(g_line, line_axis, has_before, has_after):
    length = g_line.shape[line_axis] - 2
    weight = 0.5 * (
        lax.slice_in_dim(g_line, 0, length + 1, axis=line_axis)
        + lax.slice_in_dim(g_line, 1, length + 2, axis=line_axis)
    )
    shape = [1] * weight.ndim
    shape[line_axis] = length + 1
    edge_index = lax.broadcasted_iota(jnp.int32, tuple(shape), line_axis)
    keep_mask = jnp.where(edge_index == 0, has_before, 1.0) * jnp.where(
        edge_index == length, has_after, 1.0
    )
    weight = weight * keep_mask
    low_diag = -3.0 * TIME_STEP * lax.slice_in_dim(weight, 0, length, axis=line_axis)
    high_diag = -3.0 * TIME_STEP * lax.slice_in_dim(weight, 1, length + 1, axis=line_axis)
    main_diag = 1.0 - low_diag - high_diag
    return (low_diag, main_diag, high_diag)


def pad_zero(field, line_axis):
    widths = [(0, 0)] * field.ndim
    widths[line_axis] = (1, 1)
    return jnp.pad(field, widths)


def diffusivity(extended, z_start, z_total, y_start, y_total):
    center = extended[1:-1, 1:-1]
    z_index = z_start - 1 + lax.broadcasted_iota(jnp.int32, (center.shape[0], 1, 1), 0)
    z_next = jnp.where(z_index + 1 < z_total, extended[2:, 1:-1], center)
    z_prev = jnp.where(z_index >= 1, extended[:-2, 1:-1], center)
    y_index = y_start - 1 + lax.broadcasted_iota(jnp.int32, (1, center.shape[1], 1), 1)
    y_next = jnp.where(y_index + 1 < y_total, extended[1:-1, 2:], center)
    y_prev = jnp.where(y_index >= 1, extended[1:-1, :-2], center)
    x_next = jnp.concatenate([center[:, :, 1:], center[:, :, -1:]], axis=2)
    x_prev = jnp.concatenate([center[:, :, :1], center[:, :, :-1]], axis=2)
    slope_z = (z_next - z_prev) * 0.5
    slope_y = (y_next - y_prev) * 0.5
    slope_x = (x_next - x_prev) * 0.5
    squares = slope_z * slope_z + slope_y * slope_y + slope_x * slope_x
    return 1.0 / (1.0 + squares / CONTRAST)


def line_solve(g_field, right_side, line_axis):
    low_diag, main_diag, high_diag = coefficients(pad_zero(g_field, line_axis), line_axis, 0.0, 0.0)
    return cyclic_solve(low_diag, main_diag, high_diag, right_side, line_axis, line_axis)


def on_device(volume, owners):
    field = volume
    depth, height, width = field.shape
    z_rank = lax.axis_index("gz")
    z_count = lax.axis_size("gz")
    y_rank = lax.axis_index("xy")
    y_count = lax.axis_size("xy")
    for section_index in range(STEPS):
        extended = with_halo(field, (("gz", 0), ("xy", 1)), 2)
        g_ext = diffusivity(
            extended, z_rank * depth, depth * z_count, y_rank * height, height * y_count
        )
        g_own = g_ext[1:-1, 1:-1]
        along_x = line_solve(g_own, field, 2)
        moved_g, moved_field = (
            lax.all_to_all(g_own, "xy", split_axis=0, concat_axis=1, tiled=True),
            lax.all_to_all(field, "xy", split_axis=0, concat_axis=1, tiled=True),
        )
        along_y = lax.all_to_all(
            line_solve(moved_g, moved_field, 1), "xy", split_axis=1, concat_axis=0, tiled=True
        )
        moved_g, moved_field = (
            lax.all_to_all(g_own, "gz", split_axis=1, concat_axis=0, tiled=True),
            lax.all_to_all(field, "gz", split_axis=1, concat_axis=0, tiled=True),
        )
        along_z = lax.all_to_all(
            line_solve(moved_g, moved_field, 0), "gz", split_axis=0, concat_axis=1, tiled=True
        )
        field = (along_x + along_y + along_z) / 3.0
    blocks = field.reshape(-1, BLOCK_ROWS, width)
    targets = owners.reshape(-1)
    block_count = targets.shape[0]
    same = targets[:, None] == targets[None, :]
    block_iota = jnp.arange(block_count, dtype=jnp.int32)
    earlier = block_iota[:, None] < block_iota[None, :]
    order_rank = jnp.sum((same & earlier).astype(jnp.int32), axis=0)
    slot_index = targets * MOST + order_rank
    outgoing = (
        jnp.zeros((z_count * MOST, BLOCK_ROWS, width), field.dtype).at[slot_index].set(blocks)
    )
    incoming = lax.all_to_all(outgoing, "gz", split_axis=0, concat_axis=0, tiled=True)
    return (field, incoming.reshape(1, z_count * MOST, BLOCK_ROWS, width))


def solution(mesh):
    in_specs = (P("gz", "xy", None), P("xy", "gz", None))
    out_specs = (P("gz", "xy", None), P("xy", "gz", None, None))
    return jax.shard_map(
        on_device, mesh=mesh, in_specs=in_specs, out_specs=out_specs, check_vma=False
    )
```

profile of v0, /device:TPU:0, one launch (start us, length us, event | category | flops | bytes accessed | tf_op | source)
XLA Modules:
  0.0 227.5 jit_solution(3731670692616985361)
XLA Ops:
  0.6 4.5 %all-to-all-start = ((f32[16,32,128]{2,1,0:T(8,128)}), f32[16,32,128]{2,1,0:T(8,128)S(1)}, u32[]{:S(2)}, u32[]{:S(2)}) async-start(f32[16,32,128]{2,1,0:T(8,128)} %param.2), calls=%async_computation | async-start | bytes 524288 | tf_op jit(solution)/shard_map/all_to_all | solution.py:127
  6.0 3.5 %collective-permute-start = (f32[2,32,128]{2,1,0:T(8,128)S(1)}, f32[2,32,128]{2,1,0:T(8,128)S(1)}, u32[]{:S(2)}, u32[]{:S(2)}) collective-permute-start(f32[2,32,128]{2,1,0:T(8,128)S(1)} %get-tuple-element.513), channel_id=1, source_target_pairs={{0,8},{8,16},{16,24},{24,32},{32,40},{40,48},{48,56},{56,64},{64,7... | collective-permute-start | bytes 98312 | tf_op jit(solution)/shard_map/ppermute | solution.py:20
  9.4 1.3 collective-permute-start.1
  10.8 1.2 fusion.155
  12.8 1.0 constant_dynamic-update-slice_fusion.1
  13.8 1.5 collective-permute-done.1
  15.3 1.3 collective-permute-start.3
  16.6 3.0 %collective-permute-start.2 = (f32[20,2,128]{2,1,0:T(2,128)S(1)}, f32[20,2,128]{2,1,0:T(2,128)S(1)}, u32[]{:S(2)}, u32[]{:S(2)}) collective-permute-start(f32[20,2,128]{2,1,0:T(2,128)S(1)} %get-tuple-element.154), channel_id=1, source_target_pairs={{0,1},{1,2},{2,3},{3,4},{4,5},{5,6},{6,7},{8,9},{9,10},{10,11},{11... | collective-permute-start | bytes 61448 | tf_op jit(solution)/shard_map/ppermute | solution.py:20
  22.2 1.2 fusion.1
  30.7 9.5 %all-to-all-start.3 = ((f32[16,32,128]{2,0,1:T(8,128)}), f32[16,32,128]{2,0,1:T(8,128)S(1)}, u32[]{:S(2)}, u32[]{:S(2)}) async-start(f32[16,32,128]{2,0,1:T(8,128)} %copy.53), calls=%async_computation.3 | async-start | bytes 524288 | tf_op jit(solution)/shard_map/all_to_all | solution.py:134
  40.3 1.3 pad_multiply_fusion.68
  41.6 1.8 copy.55
  43.5 6.6 %all-to-all-done.3 = f32[16,32,128]{2,0,1:T(8,128)S(1)} async-done(((f32[16,32,128]{2,0,1:T(8,128)}), f32[16,32,128]{2,0,1:T(8,128)S(1)}, u32[]{:S(2)}, u32[]{:S(2)}) %all-to-all-start.3) | async-done | bytes 262176 | tf_op jit(solution)/shard_map/all_to_all | solution.py:134
  50.1 5.5 %all-to-all-start.1 = ((f32[16,32,128]{2,1,0:T(8,128)}), f32[16,32,128]{2,1,0:T(8,128)S(1)}, u32[]{:S(2)}, u32[]{:S(2)}) async-start(f32[16,32,128]{2,1,0:T(8,128)} %fusion.26), calls=%async_computation.1 | async-start | bytes 524288 | tf_op jit(solution)/shard_map/all_to_all | solution.py:126
  55.6 7.5 %all-to-all-done.1 = f32[16,32,128]{2,1,0:T(8,128)S(1)} async-done(((f32[16,32,128]{2,1,0:T(8,128)}), f32[16,32,128]{2,1,0:T(8,128)S(1)}, u32[]{:S(2)}, u32[]{:S(2)}) %all-to-all-start.1) | async-done | bytes 262176 | tf_op jit(solution)/shard_map/all_to_all | solution.py:126
  63.1 3.7 %all-to-all-start.4 = ((f32[16,32,128]{2,0,1:T(8,128)}), f32[16,32,128]{2,0,1:T(8,128)S(1)}, u32[]{:S(2)}, u32[]{:S(2)}) async-start(f32[16,32,128]{2,0,1:T(8,128)} %copy.55), calls=%async_computation.4 | async-start | bytes 524288 | tf_op jit(solution)/shard_map/all_to_all | solution.py:133
  70.9 0.9 copy.50
  71.8 3.5 %all-to-all-done.4 = f32[16,32,128]{2,0,1:T(8,128)S(1)} async-done(((f32[16,32,128]{2,0,1:T(8,128)}), f32[16,32,128]{2,0,1:T(8,128)S(1)}, u32[]{:S(2)}, u32[]{:S(2)}) %all-to-all-start.4) | async-done | bytes 262176 | tf_op jit(solution)/shard_map/all_to_all | solution.py:133
  75.3 3.4 %all-to-all-start.2 = ((f32[2,256,128]{2,0,1:T(2,128)}), f32[2,256,128]{2,0,1:T(2,128)S(1)}, u32[]{:S(2)}, u32[]{:S(2)}) async-start(f32[2,256,128]{2,0,1:T(2,128)} %copy.50), calls=%async_computation.2 | async-start | bytes 524288 | tf_op jit(solution)/shard_map/all_to_all | solution.py:129
  83.7 2.5 %all-to-all-done.2 = f32[2,256,128]{2,0,1:T(2,128)S(1)} async-done(((f32[2,256,128]{2,0,1:T(2,128)}), f32[2,256,128]{2,0,1:T(2,128)S(1)}, u32[]{:S(2)}, u32[]{:S(2)}) %all-to-all-start.2) | async-done | bytes 262176 | tf_op jit(solution)/shard_map/all_to_all | solution.py:129
  86.2 3.5 %all-to-all-start.5 = ((f32[256,2,128]{2,1,0:T(2,128)}), f32[256,2,128]{2,1,0:T(2,128)S(1)}, u32[]{:S(2)}, u32[]{:S(2)}) async-start(f32[256,2,128]{2,1,0:T(2,128)} %copy.57), calls=%async_computation.5 | async-start | bytes 524288 | tf_op jit(solution)/shard_map/all_to_all | solution.py:136
  90.2 8.2 %all-to-all-done.5 = f32[256,2,128]{2,1,0:T(2,128)S(1)} async-done(((f32[256,2,128]{2,1,0:T(2,128)}), f32[256,2,128]{2,1,0:T(2,128)S(1)}, u32[]{:S(2)}, u32[]{:S(2)}) %all-to-all-start.5) | async-done | bytes 262176 | tf_op jit(solution)/shard_map/all_to_all | solution.py:136
  98.4 1.1 fusion.31
  100.3 1.3 collective-permute-start.5
  101.6 4.5 %collective-permute-start.4 = (f32[2,32,128]{2,1,0:T(8,128)S(1)}, f32[2,32,128]{2,1,0:T(8,128)S(1)}, u32[]{:S(2)}, u32[]{:S(2)}) collective-permute-start(f32[2,32,128]{2,1,0:T(8,128)S(1)} %get-tuple-element.338), channel_id=1, source_target_pairs={{0,8},{8,16},{16,24},{24,32},{32,40},{40,48},{48,56},{56,64},{64,7... | collective-permute-start | bytes 98312 | tf_op jit(solution)/shard_map/ppermute | solution.py:20
  106.2 3.4 %all-to-all-start.6 = ((f32[16,32,128]{2,1,0:T(8,128)}), f32[16,32,128]{2,1,0:T(8,128)S(1)}, u32[]{:S(2)}, u32[]{:S(2)}) async-start(f32[16,32,128]{2,1,0:T(8,128)} %fusion.31), calls=%async_computation.6 | async-start | bytes 524288 | tf_op jit(solution)/shard_map/all_to_all | solution.py:127
  110.5 1.3 collective-permute-start.7
  111.8 3.3 %collective-permute-start.6 = (f32[20,2,128]{2,1,0:T(2,128)S(1)}, f32[20,2,128]{2,1,0:T(2,128)S(1)}, u32[]{:S(2)}, u32[]{:S(2)}) collective-permute-start(f32[20,2,128]{2,1,0:T(2,128)S(1)} %get-tuple-element.152), channel_id=1, source_target_pairs={{0,1},{1,2},{2,3},{3,4},{4,5},{5,6},{6,7},{8,9},{9,10},{10,11},{11... | collective-permute-start | bytes 61448 | tf_op jit(solution)/shard_map/ppermute | solution.py:20
  115.1 1.2 fusion.68
  116.2 1.8 copy.66
  118.1 1.0 pad_maximum_fusion.1
  119.7 1.2 fusion.9
  121.8 1.2 fusion.3
  123.6 1.3 multiply_add_fusion.38
  131.3 5.0 %all-to-all-start.9 = ((f32[16,32,128]{2,0,1:T(8,128)}), f32[16,32,128]{2,0,1:T(8,128)S(1)}, u32[]{:S(2)}, u32[]{:S(2)}) async-start(f32[16,32,128]{2,0,1:T(8,128)} %copy.66), calls=%async_computation.9 | async-start | bytes 524288 | tf_op jit(solution)/shard_map/all_to_all | solution.py:134
  136.3 1.3 pad_multiply_fusion.28
  137.6 1.8 copy.68
  139.5 6.6 %all-to-all-done.9 = f32[16,32,128]{2,0,1:T(8,128)S(1)} async-done(((f32[16,32,128]{2,0,1:T(8,128)}), f32[16,32,128]{2,0,1:T(8,128)S(1)}, u32[]{:S(2)}, u32[]{:S(2)}) %all-to-all-start.9) | async-done | bytes 262176 | tf_op jit(solution)/shard_map/all_to_all | solution.py:134
  146.1 4.9 %all-to-all-start.7 = ((f32[16,32,128]{2,1,0:T(8,128)}), f32[16,32,128]{2,1,0:T(8,128)S(1)}, u32[]{:S(2)}, u32[]{:S(2)}) async-start(f32[16,32,128]{2,1,0:T(8,128)} %fusion.20), calls=%async_computation.7 | async-start | bytes 524288 | tf_op jit(solution)/shard_map/all_to_all | solution.py:126
  151.1 7.5 %all-to-all-done.7 = f32[16,32,128]{2,1,0:T(8,128)S(1)} async-done(((f32[16,32,128]{2,1,0:T(8,128)}), f32[16,32,128]{2,1,0:T(8,128)S(1)}, u32[]{:S(2)}, u32[]{:S(2)}) %all-to-all-start.7) | async-done | bytes 262176 | tf_op jit(solution)/shard_map/all_to_all | solution.py:126
  158.5 3.5 %all-to-all-start.10 = ((f32[16,32,128]{2,0,1:T(8,128)}), f32[16,32,128]{2,0,1:T(8,128)S(1)}, u32[]{:S(2)}, u32[]{:S(2)}) async-start(f32[16,32,128]{2,0,1:T(8,128)} %copy.68), calls=%async_computation.10 | async-start | bytes 524288 | tf_op jit(solution)/shard_map/all_to_all | solution.py:133
  167.0 3.7 %all-to-all-done.10 = f32[16,32,128]{2,0,1:T(8,128)S(1)} async-done(((f32[16,32,128]{2,0,1:T(8,128)}), f32[16,32,128]{2,0,1:T(8,128)S(1)}, u32[]{:S(2)}, u32[]{:S(2)}) %all-to-all-start.10) | async-done | bytes 262176 | tf_op jit(solution)/shard_map/all_to_all | solution.py:133
  170.7 3.7 %all-to-all-start.8 = ((f32[2,256,128]{2,0,1:T(2,128)}), f32[2,256,128]{2,0,1:T(2,128)S(1)}, u32[]{:S(2)}, u32[]{:S(2)}) async-start(f32[2,256,128]{2,0,1:T(2,128)} %copy.63), calls=%async_computation.8 | async-start | bytes 524288 | tf_op jit(solution)/shard_map/all_to_all | solution.py:129
  179.4 2.2 all-to-all-done.8
  181.6 3.5 %all-to-all-start.11 = ((f32[256,2,128]{2,1,0:T(2,128)}), f32[256,2,128]{2,1,0:T(2,128)S(1)}, u32[]{:S(2)}, u32[]{:S(2)}) async-start(f32[256,2,128]{2,1,0:T(2,128)} %copy.70), calls=%async_computation.11 | async-start | bytes 524288 | tf_op jit(solution)/shard_map/all_to_all | solution.py:136
  185.6 8.2 %all-to-all-done.11 = f32[256,2,128]{2,1,0:T(2,128)S(1)} async-done(((f32[256,2,128]{2,1,0:T(2,128)}), f32[256,2,128]{2,1,0:T(2,128)S(1)}, u32[]{:S(2)}, u32[]{:S(2)}) %all-to-all-start.11) | async-done | bytes 262176 | tf_op jit(solution)/shard_map/all_to_all | solution.py:136
  195.1 31.0 %all_to_all.221 = f32[32,128,128]{2,1,0:T(8,128)S(1)} all-to-all(f32[32,128,128]{2,1,0:T(8,128)S(1)} %scatter_fusion), channel_id=1, replica_groups=mesh['gz'=16,'xy'=8] {'gz'}, dimensions={0} | all-to-all | bytes 4194304 | tf_op jit(solution)/shard_map/all_to_all | solution.py:151
  226.1 1.3 copy.80
  (325 shorter events, 41.4 us)
Async XLA Ops:
  0.6 19.0 %copy-start = (f32[16,32,128]{2,1,0:T(8,128)S(1)}, f32[16,32,128]{2,1,0:T(8,128)}, u32[]{:S(2)}) copy-start(f32[16,32,128]{2,1,0:T(8,128)} %param.2) | copy-start | bytes 786436
  0.6 30.1 %all-to-all-start = ((f32[16,32,128]{2,1,0:T(8,128)}), f32[16,32,128]{2,1,0:T(8,128)S(1)}, u32[]{:S(2)}, u32[]{:S(2)}) async-start(f32[16,32,128]{2,1,0:T(8,128)} %param.2), calls=%async_computation | async-start | bytes 524288 | tf_op jit(solution)/shard_map/all_to_all | solution.py:127
  6.0 6.8 %collective-permute-start = (f32[2,32,128]{2,1,0:T(8,128)S(1)}, f32[2,32,128]{2,1,0:T(8,128)S(1)}, u32[]{:S(2)}, u32[]{:S(2)}) collective-permute-start(f32[2,32,128]{2,1,0:T(8,128)S(1)} %get-tuple-element.513), channel_id=1, source_target_pairs={{0,8},{8,16},{16,24},{24,32},{32,40},{40,48},{48,56},{56,64},{64,7... | collective-permute-start | bytes 98312 | tf_op jit(solution)/shard_map/ppermute | solution.py:20
  9.4 5.8 %collective-permute-start.1 = (f32[2,32,128]{2,1,0:T(8,128)S(1)}, f32[2,32,128]{2,1,0:T(8,128)S(1)}, u32[]{:S(2)}, u32[]{:S(2)}) collective-permute-start(f32[2,32,128]{2,1,0:T(8,128)S(1)} %get-tuple-element.512), channel_id=1, source_target_pairs={{8,0},{16,8},{24,16},{32,24},{40,32},{48,40},{56,48},{64,56},{72,6... | collective-permute-start | bytes 98312 | tf_op jit(solution)/shard_map/ppermute | solution.py:23
  15.3 5.2 %collective-permute-start.3 = (f32[20,2,128]{2,1,0:T(2,128)S(1)}, f32[20,2,128]{2,1,0:T(2,128)S(1)}, u32[]{:S(2)}, u32[]{:S(2)}) collective-permute-start(f32[20,2,128]{2,1,0:T(2,128)S(1)} %get-tuple-element.155), channel_id=1, source_target_pairs={{1,0},{2,1},{3,2},{4,3},{5,4},{6,5},{7,6},{9,8},{10,9},{11,10},{12... | collective-permute-start | bytes 61448 | tf_op jit(solution)/shard_map/ppermute | solution.py:23
  16.6 3.9 %collective-permute-start.2 = (f32[20,2,128]{2,1,0:T(2,128)S(1)}, f32[20,2,128]{2,1,0:T(2,128)S(1)}, u32[]{:S(2)}, u32[]{:S(2)}) collective-permute-start(f32[20,2,128]{2,1,0:T(2,128)S(1)} %get-tuple-element.154), channel_id=1, source_target_pairs={{0,1},{1,2},{2,3},{3,4},{4,5},{5,6},{6,7},{8,9},{9,10},{10,11},{11... | collective-permute-start | bytes 61448 | tf_op jit(solution)/shard_map/ppermute | solution.py:20
  30.7 19.3 %all-to-all-start.3 = ((f32[16,32,128]{2,0,1:T(8,128)}), f32[16,32,128]{2,0,1:T(8,128)S(1)}, u32[]{:S(2)}, u32[]{:S(2)}) async-start(f32[16,32,128]{2,0,1:T(8,128)} %copy.53), calls=%async_computation.3 | async-start | bytes 524288 | tf_op jit(solution)/shard_map/all_to_all | solution.py:134
  50.1 13.1 %all-to-all-start.1 = ((f32[16,32,128]{2,1,0:T(8,128)}), f32[16,32,128]{2,1,0:T(8,128)S(1)}, u32[]{:S(2)}, u32[]{:S(2)}) async-start(f32[16,32,128]{2,1,0:T(8,128)} %fusion.26), calls=%async_computation.1 | async-start | bytes 524288 | tf_op jit(solution)/shard_map/all_to_all | solution.py:126
  63.1 12.2 %all-to-all-start.4 = ((f32[16,32,128]{2,0,1:T(8,128)}), f32[16,32,128]{2,0,1:T(8,128)S(1)}, u32[]{:S(2)}, u32[]{:S(2)}) async-start(f32[16,32,128]{2,0,1:T(8,128)} %copy.55), calls=%async_computation.4 | async-start | bytes 524288 | tf_op jit(solution)/shard_map/all_to_all | solution.py:133
  75.3 10.9 %all-to-all-start.2 = ((f32[2,256,128]{2,0,1:T(2,128)}), f32[2,256,128]{2,0,1:T(2,128)S(1)}, u32[]{:S(2)}, u32[]{:S(2)}) async-start(f32[2,256,128]{2,0,1:T(2,128)} %copy.50), calls=%async_computation.2 | async-start | bytes 524288 | tf_op jit(solution)/shard_map/all_to_all | solution.py:129
  86.2 12.2 %all-to-all-start.5 = ((f32[256,2,128]{2,1,0:T(2,128)}), f32[256,2,128]{2,1,0:T(2,128)S(1)}, u32[]{:S(2)}, u32[]{:S(2)}) async-start(f32[256,2,128]{2,1,0:T(2,128)} %copy.57), calls=%async_computation.5 | async-start | bytes 524288 | tf_op jit(solution)/shard_map/all_to_all | solution.py:136
  98.4 7.7 %copy-start.2 = (s32[1,4,1]{1,2,0:T(1,128)S(1)}, s32[1,4,1]{1,2,0:T(1,128)}, u32[]{:S(2)}) copy-start(s32[1,4,1]{1,2,0:T(1,128)} %param.3) | copy-start | bytes 52
  100.3 9.3 %collective-permute-start.5 = (f32[2,32,128]{2,1,0:T(8,128)S(1)}, f32[2,32,128]{2,1,0:T(8,128)S(1)}, u32[]{:S(2)}, u32[]{:S(2)}) collective-permute-start(f32[2,32,128]{2,1,0:T(8,128)S(1)} %get-tuple-element.339), channel_id=1, source_target_pairs={{8,0},{16,8},{24,16},{32,24},{40,32},{48,40},{56,48},{64,56},{72,6... | collective-permute-start | bytes 98312 | tf_op jit(solution)/shard_map/ppermute | solution.py:23
  101.6 8.0 %collective-permute-start.4 = (f32[2,32,128]{2,1,0:T(8,128)S(1)}, f32[2,32,128]{2,1,0:T(8,128)S(1)}, u32[]{:S(2)}, u32[]{:S(2)}) collective-permute-start(f32[2,32,128]{2,1,0:T(8,128)S(1)} %get-tuple-element.338), channel_id=1, source_target_pairs={{0,8},{8,16},{16,24},{24,32},{32,40},{40,48},{48,56},{56,64},{64,7... | collective-permute-start | bytes 98312 | tf_op jit(solution)/shard_map/ppermute | solution.py:20
  106.2 25.1 %all-to-all-start.6 = ((f32[16,32,128]{2,1,0:T(8,128)}), f32[16,32,128]{2,1,0:T(8,128)S(1)}, u32[]{:S(2)}, u32[]{:S(2)}) async-start(f32[16,32,128]{2,1,0:T(8,128)} %fusion.31), calls=%async_computation.6 | async-start | bytes 524288 | tf_op jit(solution)/shard_map/all_to_all | solution.py:127
  110.5 7.5 %collective-permute-start.7 = (f32[20,2,128]{2,1,0:T(2,128)S(1)}, f32[20,2,128]{2,1,0:T(2,128)S(1)}, u32[]{:S(2)}, u32[]{:S(2)}) collective-permute-start(f32[20,2,128]{2,1,0:T(2,128)S(1)} %get-tuple-element.153), channel_id=1, source_target_pairs={{1,0},{2,1},{3,2},{4,3},{5,4},{6,5},{7,6},{9,8},{10,9},{11,10},{12... | collective-permute-start | bytes 61448 | tf_op jit(solution)/shard_map/ppermute | solution.py:23
  111.8 6.2 %collective-permute-start.6 = (f32[20,2,128]{2,1,0:T(2,128)S(1)}, f32[20,2,128]{2,1,0:T(2,128)S(1)}, u32[]{:S(2)}, u32[]{:S(2)}) collective-permute-start(f32[20,2,128]{2,1,0:T(2,128)S(1)} %get-tuple-element.152), channel_id=1, source_target_pairs={{0,1},{1,2},{2,3},{3,4},{4,5},{5,6},{6,7},{8,9},{9,10},{10,11},{11... | collective-permute-start | bytes 61448 | tf_op jit(solution)/shard_map/ppermute | solution.py:20
  131.3 14.8 %all-to-all-start.9 = ((f32[16,32,128]{2,0,1:T(8,128)}), f32[16,32,128]{2,0,1:T(8,128)S(1)}, u32[]{:S(2)}, u32[]{:S(2)}) async-start(f32[16,32,128]{2,0,1:T(8,128)} %copy.66), calls=%async_computation.9 | async-start | bytes 524288 | tf_op jit(solution)/shard_map/all_to_all | solution.py:134
  146.1 12.5 %all-to-all-start.7 = ((f32[16,32,128]{2,1,0:T(8,128)}), f32[16,32,128]{2,1,0:T(8,128)S(1)}, u32[]{:S(2)}, u32[]{:S(2)}) async-start(f32[16,32,128]{2,1,0:T(8,128)} %fusion.20), calls=%async_computation.7 | async-start | bytes 524288 | tf_op jit(solution)/shard_map/all_to_all | solution.py:126
  158.5 12.2 %all-to-all-start.10 = ((f32[16,32,128]{2,0,1:T(8,128)}), f32[16,32,128]{2,0,1:T(8,128)S(1)}, u32[]{:S(2)}, u32[]{:S(2)}) async-start(f32[16,32,128]{2,0,1:T(8,128)} %copy.68), calls=%async_computation.10 | async-start | bytes 524288 | tf_op jit(solution)/shard_map/all_to_all | solution.py:133
  170.7 10.9 %all-to-all-start.8 = ((f32[2,256,128]{2,0,1:T(2,128)}), f32[2,256,128]{2,0,1:T(2,128)S(1)}, u32[]{:S(2)}, u32[]{:S(2)}) async-start(f32[2,256,128]{2,0,1:T(2,128)} %copy.63), calls=%async_computation.8 | async-start | bytes 524288 | tf_op jit(solution)/shard_map/all_to_all | solution.py:129
  181.6 12.2 %all-to-all-start.11 = ((f32[256,2,128]{2,1,0:T(2,128)}), f32[256,2,128]{2,1,0:T(2,128)S(1)}, u32[]{:S(2)}, u32[]{:S(2)}) async-start(f32[256,2,128]{2,1,0:T(2,128)} %copy.70), calls=%async_computation.11 | async-start | bytes 524288 | tf_op jit(solution)/shard_map/all_to_all | solution.py:136
  194.2 31.9 %copy-start.1 = (f32[16,32,128]{2,1,0:T(8,128)}, f32[16,32,128]{2,1,0:T(8,128)S(1)}, u32[]{:S(2)}) copy-start(f32[16,32,128]{2,1,0:T(8,128)S(1)} %fusion.29) | copy-start | bytes 786436
where the time goes:
time: 229 us; the launch traced here: 227 us
  starting transfers between devices  73.8 us (32%)
  waiting for transfers between devices  57.8 us (25%)
  other arithmetic  31.5 us (14%)
  blocking collectives  31 us (14%)
  local copies, waits for them, and re-layouts  30.5 us (13%)
  between operations  2.79 us (1%)
    all_to_all x1, blocking collectives, on_device(): lax.all_to_all(outgoing, 'gz', split_axis=0, concat_axis=0, tiled=True)  31 us
    all_to_all x2, waiting for transfers between devices, on_device(): lax.all_to_all(line_solve(moved_g, moved_field, 0), 'gz', split_axis=0, c...  16.4 us
    all_to_all x2, waiting for transfers between devices, on_device(): lax.all_to_all(g_own, 'xy', split_axis=0, concat_axis=1, tiled=True)  14.9 us
    all_to_all x2, starting transfers between devices, on_device(): lax.all_to_all(field, 'gz', split_axis=1, concat_axis=0, tiled=True)  14.6 us
    ppermute x4, starting transfers between devices, with_halo(): lax.ppermute(lax.slice_in_dim(block, block.shape[dim] - width, None, axis...  14.3 us
    all_to_all x2, waiting for transfers between devices, on_device(): lax.all_to_all(field, 'gz', split_axis=1, concat_axis=0, tiled=True)  13.2 us
    all_to_all x2, starting transfers between devices, on_device(): lax.all_to_all(g_own, 'xy', split_axis=0, concat_axis=1, tiled=True)  10.4 us
    add x34, other arithmetic, cyclic_solve(): right_side = right_side + factor_low * side_prev + factor_high * side_next  9.31 us
  transfers between devices with their start and end apart: 20, of which 11 were waited for; matrix products, arithmetic and copies ran while one was open for 25% of the time, Pallas kernels for 0%

commit v1 on v0

v1 whole, which is shorter than its diff:
```python
import jax
import jax.numpy as jnp
from jax import lax
from jax.experimental import pallas as pl
from jax.experimental.pallas import tpu as pltpu
from jax.sharding import PartitionSpec as P

STEPS = 2
MOST = 2
BLOCK_ROWS = 128

TIME_STEP = 30.0
CONTRAST = 4.0
HALF_K = 1.5 * TIME_STEP

CZ = 16
CY = 32
NX = 128
ROWS = CZ * CY
N_GZ = 16
N_XY = 8
FIELDS = 7
MESH = pl.DeviceIdType.MESH

Z_PEERS = sorted(
    [(a, b) for a in range(4) for b in range(4) if (a, b) != (0, 0)],
    key=lambda p: -(min(p[0], 4 - p[0]) + min(p[1], 4 - p[1])),
)
Y_PEERS = sorted(
    [(a, b) for a in range(4) for b in range(2) if (a, b) != (0, 0)],
    key=lambda p: -(2 * min(p[0], 4 - p[0]) + p[1]),
)


def recip(value):
    return 1.0 / value


def pcr(diag, coupling, side, count, axis):
    stride = 1
    while stride < count:
        inverse = recip(diag)
        scaled = coupling * inverse
        side_scaled = side * inverse
        side = (
            side
            + pltpu.roll(coupling * side_scaled, stride, axis)
            + coupling * pltpu.roll(side_scaled, count - stride, axis)
        )
        diag = (
            diag
            - pltpu.roll(coupling * scaled, stride, axis)
            - coupling * coupling * pltpu.roll(inverse, count - stride, axis)
        )
        stride *= 2
        if stride < count:
            coupling = coupling * pltpu.roll(scaled, count - stride // 2, axis)
    return side * recip(diag)


def forward_sweep(count, load_v, load_g, store):
    g_here = load_g(0)
    g_first = g_here
    total = jnp.ones_like(g_here)
    side = load_v(0)
    unit = jnp.ones_like(g_here)
    first_side = jnp.zeros_like(g_here)
    first_unit = jnp.zeros_like(g_here)
    for i in range(count - 1):
        g_next = load_g(i + 1)
        weight = HALF_K * (g_here + g_next)
        inverse = recip(total + weight)
        ratio = weight * inverse
        side_scaled = side * inverse
        unit_scaled = unit * inverse
        store(i, ratio, side_scaled, unit_scaled)
        first_side = first_side + unit * side_scaled
        first_unit = first_unit + unit * unit_scaled
        total = 1.0 + ratio * total
        side = load_v(i + 1) + ratio * side
        unit = ratio * unit
        g_here = g_next
    inverse = recip(total)
    last_side = side * inverse
    last_unit = unit * inverse
    store(count - 1, inverse, last_side, last_unit)
    first_side = first_side + unit * last_side
    first_unit = first_unit + unit * last_unit
    return (first_side, last_side, first_unit, last_unit, inverse, g_first, g_here)


def backward_sweep(count, load, store):
    high_unit, side, low_unit = load(count - 1)
    store(count - 1, side, low_unit, high_unit)
    for i in range(count - 2, -1, -1):
        ratio, side_scaled, unit_scaled = load(i)
        side = side_scaled + ratio * side
        low_unit = unit_scaled + ratio * low_unit
        high_unit = ratio * high_unit
        store(i, side, low_unit, high_unit)


def interface_fluxes(received, count, half):
    first_side, last_side, first_unit, cross, last_unit, g_first, g_last = [received(j) for j in range(FIELDS)]
    index = lax.broadcasted_iota(jnp.int32, (count, NX), 0)

    def following(field):
        return pltpu.roll(field, count - 1, 0)

    weight = HALF_K * (g_last + following(g_first))
    diag = recip(weight) + last_unit + following(first_unit)
    side = last_side - following(first_side)
    diag = jnp.where(index < count - 1, diag, 1.0)
    side = jnp.where(index < count - 1, side, 0.0)
    coupling = jnp.where(index < count - 2, following(cross), 0.0)
    return pcr(diag, coupling, side, count, 0)


def solver_kernel(
    volume_ref,
    out_ref,
    middle,
    z_halo,
    y_halo_out,
    y_halo,
    g_ref,
    z_keep,
    y_keep,
    natural,
    base,
    z_out,
    z_in,
    y_out,
    y_in,
    z_back_out,
    z_back,
    y_back_out,
    y_back,
    halo_send,
    halo_recv,
    z_send,
    z_recv,
    y_send,
    y_recv,
    zb_send,
    zb_recv,
    yb_send,
    yb_recv,
):
    gz = lax.axis_index("gz")
    xy = lax.axis_index("xy")
    z_targets = [
        lax.rem(gz // 4 + dz, 4) * 4 + lax.rem(lax.rem(gz, 4) + dy, 4) for dz, dy in Z_PEERS
    ]
    y_targets = [
        lax.rem(xy // 2 + dx, 4) * 2 + lax.rem(lax.rem(xy, 2) + core, 2) for dx, core in Y_PEERS
    ]
    barrier = pltpu.get_barrier_semaphore()
    for target in z_targets:
        pl.semaphore_signal(barrier, 1, device_id={"gz": target}, device_id_type=MESH)
    for target in y_targets:
        pl.semaphore_signal(barrier, 1, device_id={"xy": target}, device_id_type=MESH)
    pl.semaphore_wait(barrier, N_GZ + N_XY - 2)

    row_index = lax.broadcasted_iota(jnp.int32, (CY, NX), 0)
    lane_index = lax.broadcasted_iota(jnp.int32, (CY, NX), 1)

    def send_all(source, landing, send_sem, recv_sem, axis, targets, me):
        for target in targets:
            pltpu.make_async_remote_copy(
                source.at[target], landing.at[me], send_sem, recv_sem,
                device_id={axis: target}, device_id_type=MESH,
            ).start()

    def wait_all(buffer, count, semaphore):
        part = buffer.at[pl.ds(0, count)]
        pltpu.make_async_copy(part, part, semaphore).wait()

    for step in range(STEPS):
        v = volume_ref if step == 0 else middle
        new = out_ref if step == STEPS - 1 else middle

        y_halo_out[step, 0] = v[pl.ds(0, CZ, stride=CY), :]
        y_halo_out[step, 1] = v[pl.ds(CY - 1, CZ, stride=CY), :]
        copies = []
        for k, (axis, me, count, forward) in enumerate(
            [("gz", gz, N_GZ, 0), ("gz", gz, N_GZ, 1), ("xy", xy, N_XY, 0), ("xy", xy, N_XY, 1)]
        ):
            target = lax.rem(me + (1 if forward else count - 1), count)
            if axis == "gz":
                source = v.at[pl.ds((CZ - 1) * CY if forward else 0, CY)]
                landing = z_halo.at[step, 1 - forward]
            else:
                source = y_halo_out.at[step, forward]
                landing = y_halo.at[step, 1 - forward]
            copies.append(
                pltpu.make_async_remote_copy(
                    source, landing, halo_send.at[step, k], halo_recv.at[step, k],
                    device_id={axis: target}, device_id_type=MESH,
                )
            )
        for copy in copies:
            copy.start()
        for copy in copies:
            copy.wait_recv()

        def plane(i):
            return v[i * CY : (i + 1) * CY, :]

        before = jnp.where(gz == 0, plane(0), z_halo[step, 0])
        after = jnp.where(gz == N_GZ - 1, plane(CZ - 1), z_halo[step, 1])
        here = plane(0)
        for i in range(CZ):
            above = plane(i + 1) if i < CZ - 1 else after
            slope_z = above - before
            y_low = jnp.where(xy == 0, here[0:1, :], y_halo[step, 0, i : i + 1, :])
            y_high = jnp.where(xy == N_XY - 1, here[CY - 1 : CY, :], y_halo[step, 1, i : i + 1, :])
            y_prev = jnp.where(row_index == 0, y_low, pltpu.roll(here, 1, 0))
            y_next = jnp.where(row_index == CY - 1, y_high, pltpu.roll(here, CY - 1, 0))
            slope_y = y_next - y_prev
            x_prev = jnp.where(lane_index == 0, here, pltpu.roll(here, 1, 1))
            x_next = jnp.where(lane_index == NX - 1, here, pltpu.roll(here, NX - 1, 1))
            slope_x = x_next - x_prev
            squares = slope_z * slope_z + slope_y * slope_y + slope_x * slope_x
            g_ref[i * CY : (i + 1) * CY, :] = recip(1.0 + squares * (0.25 / CONTRAST))
            before, here = here, above

        def z_store(i, ratio, side, unit):
            z_keep[0, i] = ratio
            z_keep[1, i] = side
            z_keep[2, i] = unit

        ends = forward_sweep(CZ, plane, lambda i: g_ref[i * CY : (i + 1) * CY, :], z_store)
        for j, field in enumerate(ends):
            for half in range(2):
                z_out[step, pl.ds(2 * j + half, N_GZ, stride=16), :] = field[half * N_GZ : (half + 1) * N_GZ, :]
        z_in_blocks = z_in.at[step].reshape(N_GZ, 16, NX)
        z_out_blocks = z_out.at[step].reshape(N_GZ, 16, NX)
        send_all(z_out_blocks, z_in_blocks, z_send.at[step], z_recv.at[step], "gz", z_targets, gz)

        def y_store(i, ratio, side, unit):
            y_keep[0, i] = ratio
            y_keep[1, i] = side
            y_keep[2, i] = unit

        ends = forward_sweep(
            CY,
            lambda i: v[pl.ds(i, CZ, stride=CY), :],
            lambda i: g_ref[pl.ds(i, CZ, stride=CY), :],
            y_store,
        )
        for j, field in enumerate(ends):
            for half in range(2):
                y_out[step, pl.ds(2 * j + half, N_XY, stride=16), :] = field[half * N_XY : (half + 1) * N_XY, :]
        y_in_blocks = y_in.at[step].reshape(N_XY, 16, NX)
        y_out_blocks = y_out.at[step].reshape(N_XY, 16, NX)
        send_all(y_out_blocks, y_in_blocks, y_send.at[step], y_recv.at[step], "xy", y_targets, xy)
        z_in_blocks[gz] = z_out_blocks[gz]
        y_in_blocks[xy] = y_out_blocks[xy]

        def solve_x(i, carry):
            rows = pl.ds(pl.multiple_of(i * 2 * CY, 2 * CY), 2 * CY)
            g = g_ref[rows, :]
            lanes = lax.broadcasted_iota(jnp.int32, (2 * CY, NX), 1)
            weight = jnp.where(lanes < NX - 1, HALF_K * (g + pltpu.roll(g, NX - 1, 1)), 0.0)
            diag = 1.0 + weight + pltpu.roll(weight, 1, 1)
            base[rows, :] = pcr(diag, weight, v[rows, :], NX, 1)
            return carry

        lax.fori_loop(0, CZ // 2, solve_x, 0)

        def z_load(i):
            return z_keep[0, i], z_keep[1, i], z_keep[2, i]

        def z_restore(i, side, low, high):
            base[i * CY : (i + 1) * CY, :] += side
            z_keep[1, i] = low
            z_keep[2, i] = high

        backward_sweep(CZ, z_load, z_restore)

        def y_load(i):
            return y_keep[0, i], y_keep[1, i], y_keep[2, i]

        def y_restore(i, side, low, high):
            rows = pl.ds(i, CZ, stride=CY)
            natural[0, rows, :] = side
            natural[1, rows, :] = low
            natural[2, rows, :] = high

        backward_sweep(CY, y_load, y_restore)

        wait_all(z_in_blocks, N_GZ - 1, z_recv.at[step])
        zb_out = z_back_out.at[step].reshape(N_GZ, 8, NX)
        zb_in = z_back.at[step].reshape(N_GZ, 8, NX)
        for half in range(2):
            flux = interface_fluxes(
                lambda j: z_in[step, pl.ds(2 * j + half, N_GZ, stride=16), :], N_GZ, half
            )
            z_back_out[step, pl.ds(half, N_GZ, stride=8), :] = pltpu.roll(flux, 1, 0)
            z_back_out[step, pl.ds(2 + half, N_GZ, stride=8), :] = flux
        send_all(zb_out, zb_in, zb_send.at[step], zb_recv.at[step], "gz", z_targets, gz)
        zb_in[gz] = zb_out[gz]

        wait_all(y_in_blocks, N_XY - 1, y_recv.at[step])
        yb_out = y_back_out.at[step].reshape(N_XY, 8, NX)
        yb_in = y_back.at[step].reshape(N_XY, 8, NX)
        for half in range(2):
            flux = interface_fluxes(
                lambda j: y_in[step, pl.ds(2 * j + half, N_XY, stride=16), :], N_XY, half
            )
            y_back_out[step, pl.ds(half, N_XY, stride=8), :] = pltpu.roll(flux, 1, 0)
            y_back_out[step, pl.ds(2 + half, N_XY, stride=8), :] = flux
        send_all(yb_out, yb_in, yb_send.at[step], yb_recv.at[step], "xy", y_targets, xy)
        yb_in[xy] = yb_out[xy]

        wait_all(yb_in, N_XY - 1, yb_recv.at[step])
        wait_all(zb_in, N_GZ - 1, zb_recv.at[step])
        low_z = jnp.concatenate([z_back[step, pl.ds(h, N_GZ, stride=8), :] for h in (0, 1)], axis=0)
        high_z = jnp.concatenate([z_back[step, pl.ds(2 + h, N_GZ, stride=8), :] for h in (0, 1)], axis=0)
        for i in range(CZ):
            rows = slice(i * CY, (i + 1) * CY)
            at = (i % N_XY) * 8 + i // N_XY
            low_y = y_back[step, at : at + 1, :]
            high_y = y_back[step, at + 2 : at + 3, :]
            total = base[rows, :] + natural[0, rows, :]
            total = total + (low_z * z_keep[1, i] - high_z * z_keep[2, i])
            total = total + (low_y * natural[1, rows, :] - high_y * natural[2, rows, :])
            new[rows, :] = total * (1.0 / 3.0)

        if step == STEPS - 1:
            continue

    for step in range(STEPS):
        v = volume_ref if step == 0 else middle
        for k in range(4):
            part = v.at[pl.ds(0, CY)] if k < 2 else y_halo_out.at[step, 0]
            pltpu.make_async_copy(part, part, halo_send.at[step, k]).wait()
        wait_all(z_out.at[step].reshape(N_GZ, 16, NX), N_GZ - 1, z_send.at[step])
        wait_all(y_out.at[step].reshape(N_XY, 16, NX), N_XY - 1, y_send.at[step])
        wait_all(z_back_out.at[step].reshape(N_GZ, 8, NX), N_GZ - 1, zb_send.at[step])
        wait_all(y_back_out.at[step].reshape(N_XY, 8, NX), N_XY - 1, yb_send.at[step])


def vmem(*shape):
    return pltpu.VMEM(shape, jnp.float32)


def solve(volume):
    dma = pltpu.SemaphoreType.DMA
    return pl.pallas_call(
        solver_kernel,
        out_shape=jax.ShapeDtypeStruct((ROWS, NX), jnp.float32),
        in_specs=[pl.BlockSpec(memory_space=pltpu.VMEM)],
        out_specs=pl.BlockSpec(memory_space=pltpu.VMEM),
        scratch_shapes=[
            vmem(ROWS, NX),
            vmem(STEPS, 2, CY, NX),
            vmem(STEPS, 2, CZ, NX),
            vmem(STEPS, 2, CZ, NX),
            vmem(ROWS, NX),
            vmem(3, CZ, CY, NX),
            vmem(3, CY, CZ, NX),
            vmem(3, ROWS, NX),
            vmem(ROWS, NX),
            vmem(STEPS, N_GZ * 16, NX),
            vmem(STEPS, N_GZ * 16, NX),
            vmem(STEPS, N_XY * 16, NX),
            vmem(STEPS, N_XY * 16, NX),
            vmem(STEPS, N_GZ * 8, NX),
            vmem(STEPS, N_GZ * 8, NX),
            vmem(STEPS, N_XY * 8, NX),
            vmem(STEPS, N_XY * 8, NX),
            dma((STEPS, 4)),
            dma((STEPS, 4)),
        ]
        + [dma((STEPS,))] * 8,
        compiler_params=pltpu.CompilerParams(
            collective_id=0, has_side_effects=True, vmem_limit_bytes=32 << 20
        ),
    )(volume)


def on_device(volume, owners):
    depth, height, width = volume.shape
    z_count = lax.axis_size("gz")
    field = solve(volume.reshape(depth * height, width))
    blocks = field.reshape(-1, BLOCK_ROWS, width)
    targets = owners.reshape(-1)
    block_count = targets.shape[0]
    same = targets[:, None] == targets[None, :]
    block_iota = jnp.arange(block_count, dtype=jnp.int32)
    earlier = block_iota[:, None] < block_iota[None, :]
    order_rank = jnp.sum((same & earlier).astype(jnp.int32), axis=0)
    slot_index = targets * MOST + order_rank
    outgoing = (
        jnp.zeros((z_count * MOST, BLOCK_ROWS, width), field.dtype).at[slot_index].set(blocks)
    )
    incoming = lax.all_to_all(outgoing, "gz", split_axis=0, concat_axis=0, tiled=True)
    return (field.reshape(volume.shape), incoming.reshape(1, z_count * MOST, BLOCK_ROWS, width))


def solution(mesh):
    in_specs = (P("gz", "xy", None), P("xy", "gz", None))
    out_specs = (P("gz", "xy", None), P("xy", "gz", None, None))
    return jax.shard_map(
        on_device, mesh=mesh, in_specs=in_specs, out_specs=out_specs, check_vma=False
    )
```

time: 229 us -> 85.6 us (0.37)
  starting transfers between devices: 73.8 us -> 5.02 us
  Pallas kernels: 0 us -> 40.6 us
  blocking collectives: 31 us -> 0 us
  other arithmetic: 31.5 us -> 1.47 us
  waiting for transfers between devices: 57.8 us -> 30.8 us
  local copies, waits for them, and re-layouts: 30.5 us -> 6.72 us
    all_to_all x12 -> x1, starting transfers between devices: 54.3 us -> 5.02 us  [on_device(): lax.all_to_all(outgoing, 'gz', split_axis=0, concat_axis=0, tiled=True)]
    pallas_call x0 -> x1, Pallas kernels: none -> 40.6 us  [solve(): pl.pallas_call(solver_kernel, out_shape=jax.ShapeDtypeStruct((ROWS, NX),...]
    all_to_all x1 -> x0, blocking collectives: 31 us -> none  [on_device(): lax.all_to_all(outgoing, 'gz', split_axis=0, concat_axis=0, tiled=True)]
    all_to_all x12 -> x1, waiting for transfers between devices: 56.3 us -> 30.8 us  [on_device(): lax.all_to_all(outgoing, 'gz', split_axis=0, concat_axis=0, tiled=True)]
    slice x191 -> x0, local copies, waits for them, and re-layouts: 20.7 us -> none  [the longest x90 7.52 us: shifted(): lax.slice_in_dim(field, 0, length - stride, axis=line_axis)]
    ppermute x8 -> x0, starting transfers between devices: 19.5 us -> none  [the longest x4 14.3 us: with_halo(): lax.ppermute(lax.slice_in_dim(block, block.shape[dim] - width, None, axis...]
    add x68 -> x0, other arithmetic: 16.5 us -> none  [the longest x34 9.31 us: cyclic_solve(): right_side = right_side + factor_low * side_prev + factor_high * side_next]
    mul x22 -> x0, other arithmetic: 7.96 us -> none  [the longest x6 3.13 us: cyclic_solve(): high_diag = factor_high * high_next]
  transfers between devices with their start and end apart: 20 -> 1, of which waited for: 11 -> 1; matrix products, arithmetic and copies ran while one was open for 25% -> 0% of each run, Pallas kernels for 0% -> 0%
where the time goes in v1:
time: 85.6 us; the launch traced here: 85.4 us
  Pallas kernels  40.6 us (47%)
  waiting for transfers between devices  30.8 us (36%)
  local copies, waits for them, and re-layouts  6.72 us (8%)
  starting transfers between devices  5.02 us (6%)
  other arithmetic  1.47 us (2%)
    pallas_call x1, Pallas kernels, solve(): pl.pallas_call(solver_kernel, out_shape=jax.ShapeDtypeStruct((ROWS, NX),...  40.6 us
    all_to_all x1, waiting for transfers between devices, on_device(): lax.all_to_all(outgoing, 'gz', split_axis=0, concat_axis=0, tiled=True)  30.8 us
    all_to_all x1, starting transfers between devices, on_device(): lax.all_to_all(outgoing, 'gz', split_axis=0, concat_axis=0, tiled=True)  5.02 us
    unnamed x4, local copies, waits for them, and re-layouts  2.96 us
    scatter x1, local copies, waits for them, and re-layouts, on_device(): jnp.zeros((z_count * MOST, BLOCK_ROWS, width), field.dtype).at[slot_index]  2.2 us
  transfers between devices with their start and end apart: 1, of which 1 were waited for; matrix products, arithmetic and copies ran while one was open for 0% of the time, Pallas kernels for 0%

profile of v1, /device:TPU:0, one launch (start us, length us, event | category | flops | bytes accessed | tf_op | source)
XLA Modules:
  0.0 85.4 jit_solution(5498158495777202672)
XLA Ops:
  0.6 0.0 copy-start
  0.6 0.9 %copy-done = f32[16,32,128]{2,1,0:T(8,128)S(1)} copy-done((f32[16,32,128]{2,1,0:T(8,128)S(1)}, f32[16,32,128]{2,1,0:T(8,128)}, u32[]{:S(2)}) %copy-start) | copy-done | bytes 262168
  1.6 40.6 %shard_map.41 = f32[512,128]{1,0:T(8,128)S(1)} custom-call(f32[512,128]{1,0:T(8,128)S(1)} %bitcast.15), custom_call_target="tpu_custom_call" | custom-call | tf_op jit(solution)/shard_map/pallas_call | solution.py:351
  42.2 0.8 convert_reduce_fusion
  43.1 0.7 fusion.1
  43.7 1.6 %broadcast_in_dim.2 = f32[32,128,128]{2,1,0:T(8,128)} broadcast(f32[]{:T(128)} %constant.4.clone.1), dimensions={} | broadcast | bytes 2097156 | tf_op jit(solution)/shard_map/broadcast_in_dim | solution.py:397
  45.3 2.2 %scatter_fusion = f32[32,128,128]{2,1,0:T(8,128)} fusion(f32[32,128,128]{2,1,0:T(8,128)} %broadcast_in_dim.2, s32[4]{0:T(128)S(1)} %fusion.1, f32[4,128,128]{2,1,0:T(8,128)S(1)} %bitcast.13), kind=kCustom, calls=%fused_computation | custom fusion | bytes 786448 | tf_op jit(solution)/shard_map/scatter | solution.py:397
  47.5 5.0 %all-to-all-start = ((f32[32,128,128]{2,1,0:T(8,128)}), f32[32,128,128]{2,1,0:T(8,128)S(1)}, u32[]{:S(2)}, u32[]{:S(2)}) async-start(f32[32,128,128]{2,1,0:T(8,128)} %scatter_fusion), calls=%async_computation | async-start | bytes 4194304 | tf_op jit(solution)/shard_map/all_to_all | solution.py:399
  52.5 30.8 %all-to-all-done = f32[32,128,128]{2,1,0:T(8,128)S(1)} async-done(((f32[32,128,128]{2,1,0:T(8,128)}), f32[32,128,128]{2,1,0:T(8,128)S(1)}, u32[]{:S(2)}, u32[]{:S(2)}) %all-to-all-start) | async-done | bytes 2097184 | tf_op jit(solution)/shard_map/all_to_all | solution.py:399
  83.3 0.7 copy.7
  84.0 1.3 %copy.8 = f32[1,32,128,128]{3,2,1,0:T(8,128)} copy(f32[1,32,128,128]{3,2,1,0:T(8,128)S(1)} %bitcast.16) | data formatting | bytes 4194304
Async XLA Ops:
  0.6 1.0 %copy-start = (f32[16,32,128]{2,1,0:T(8,128)S(1)}, f32[16,32,128]{2,1,0:T(8,128)}, u32[]{:S(2)}) copy-start(f32[16,32,128]{2,1,0:T(8,128)} %param.2) | copy-start | bytes 786436
  47.5 35.9 %all-to-all-start = ((f32[32,128,128]{2,1,0:T(8,128)}), f32[32,128,128]{2,1,0:T(8,128)S(1)}, u32[]{:S(2)}, u32[]{:S(2)}) async-start(f32[32,128,128]{2,1,0:T(8,128)} %scatter_fusion), calls=%async_computation | async-start | bytes 4194304 | tf_op jit(solution)/shard_map/all_to_all | solution.py:399

commit v2 on v1

--- a/solution.py
+++ b/solution.py
@@ -20,6 +20,10 @@
 N_GZ = 16
 N_XY = 8
 FIELDS = 7
+BLOCKS_HERE = 4
+HALF_ROWS = BLOCK_ROWS // 2
+CHUNKS = 2
+CHUNK_ROWS = HALF_ROWS // CHUNKS
 MESH = pl.DeviceIdType.MESH
 
 Z_PEERS = sorted(
@@ -116,9 +120,12 @@
     return pcr(diag, coupling, side, count, 0)
 
 
-def solver_kernel(
+def diffuse_and_route_kernel(
+    volume_hbm,
+    owners_ref,
+    out_ref,
+    routed_ref,
     volume_ref,
-    out_ref,
     middle,
     z_halo,
     y_halo_out,
@@ -146,7 +153,23 @@
     zb_recv,
     yb_send,
     yb_recv,
+    codes_out,
+    codes_in,
+    codes,
+    gathered,
+    packed,
+    volume_sem,
+    codes_send,
+    codes_recv,
+    codes_sem,
+    own_sem,
+    gather_send,
+    gather_recv,
+    spread_send,
+    spread_recv,
 ):
+    load_volume = pltpu.make_async_copy(volume_hbm, volume_ref, volume_sem)
+    load_volume.start()
     gz = lax.axis_index("gz")
     xy = lax.axis_index("xy")
     z_targets = [
@@ -161,6 +184,32 @@
     for target in y_targets:
         pl.semaphore_signal(barrier, 1, device_id={"xy": target}, device_id_type=MESH)
     pl.semaphore_wait(barrier, N_GZ + N_XY - 2)
+
+    chip_z, chip_y = gz // 4, lax.rem(gz, 4)
+    places = [chip_y, chip_z]
+
+    def partner(way, offset):
+        if way == 0:
+            return chip_z * 4 + lax.rem(chip_y + offset, 4)
+        return lax.rem(chip_z + offset, 4) * 4 + chip_y
+
+    own_codes = []
+    lanes = lax.broadcasted_iota(jnp.int32, (8, NX), 1)
+    code_tile = jnp.zeros((8, NX), jnp.int32)
+    for b in range(BLOCKS_HERE):
+        rank = 0
+        for earlier in range(b):
+            rank = rank + (owners_ref[earlier] == owners_ref[b]).astype(jnp.int32)
+        code_tile = jnp.where(lanes == b, owners_ref[b] * MOST + rank, code_tile)
+    codes_out[...] = code_tile
+    for way in range(2):
+        codes_in[way, places[way]] = code_tile
+        for offset in (2, 1, 3):
+            pltpu.make_async_remote_copy(
+                codes_out, codes_in.at[way, places[way]], codes_send.at[way], codes_recv.at[way],
+                device_id={"gz": partner(way, offset)}, device_id_type=MESH,
+            ).start()
+    load_volume.wait()
 
     row_index = lax.broadcasted_iota(jnp.int32, (CY, NX), 0)
     lane_index = lax.broadcasted_iota(jnp.int32, (CY, NX), 1)
@@ -328,9 +377,70 @@
             total = total + (low_y * natural[1, rows, :] - high_y * natural[2, rows, :])
             new[rows, :] = total * (1.0 / 3.0)
 
-        if step == STEPS - 1:
-            continue
-
+    for way in range(2):
+        wait_all(codes_in.at[way], 3, codes_recv.at[way])
+    to_scalars = pltpu.make_async_copy(codes_in, codes, codes_sem)
+    to_scalars.start()
+    blocks = out_ref.reshape(BLOCKS_HERE, BLOCK_ROWS, NX)
+    for chunk in range(CHUNKS):
+        for way in range(2):
+            here = pl.ds(way * HALF_ROWS + chunk * CHUNK_ROWS, CHUNK_ROWS)
+            for offset in (2, 1, 3):
+                pltpu.make_async_remote_copy(
+                    blocks.at[:, here, :], gathered[way][chunk].at[places[way]],
+                    gather_send.at[chunk, way], gather_recv.at[chunk, way],
+                    device_id={"gz": partner(way, offset)}, device_id_type=MESH,
+                ).start()
+    for way in range(2):
+        for chunk in range(CHUNKS):
+            here = pl.ds(way * HALF_ROWS + chunk * CHUNK_ROWS, CHUNK_ROWS)
+            gathered[way][chunk][places[way]] = blocks[:, here, :]
+    to_scalars.wait()
+    choice = {}
+    for way in range(2):
+        for offset in range(4):
+            target = partner(1 - way, offset)
+            for source in range(4):
+                for rank in range(MOST):
+                    index, found = 0, 0
+                    for b in range(BLOCKS_HERE):
+                        hit = (codes[way, source, 0, b] == target * MOST + rank).astype(jnp.int32)
+                        index = index + b * hit
+                        found = found + hit
+                    choice[way, offset, source, rank] = index, found
+    for chunk in range(CHUNKS):
+        for way in range(2):
+            there = pl.ds(chunk * CHUNK_ROWS, CHUNK_ROWS)
+            final = pl.ds(way * HALF_ROWS + chunk * CHUNK_ROWS, CHUNK_ROWS)
+            wait_all(gathered[way][chunk], 3, gather_recv.at[chunk, way])
+            for offset in (2, 1, 3, 0):
+                for source in range(4):
+                    for rank in range(MOST):
+                        index, found = choice[way, offset, source, rank]
+                        rows = gathered[way][chunk][source, index]
+                        packed[way, offset, source, rank, there, :] = jnp.where(found > 0, rows, 0.0)
+                landing = routed_ref.at[chip_z, :, :, final, :] if way == 0 else routed_ref.at[:, chip_y, :, final, :]
+                if offset:
+                    pltpu.make_async_remote_copy(
+                        packed.at[way, offset, :, :, there, :], landing,
+                        spread_send.at[chunk, way], spread_recv.at[chunk, way],
+                        device_id={"gz": partner(1 - way, offset)}, device_id_type=MESH,
+                    ).start()
+                else:
+                    pltpu.make_async_copy(
+                        packed.at[way, offset, :, :, there, :], landing, own_sem.at[chunk, way]
+                    ).start()
+    for chunk in range(CHUNKS):
+        for way in range(2):
+            there = pl.ds(chunk * CHUNK_ROWS, CHUNK_ROWS)
+            part = packed.at[way, pl.ds(0, 3), :, :, there, :]
+            pltpu.make_async_copy(part, part, spread_recv.at[chunk, way]).wait()
+            pltpu.make_async_copy(part, part, spread_send.at[chunk, way]).wait()
+            part = packed.at[way, 0, :, :, there, :]
+            pltpu.make_async_copy(part, part, own_sem.at[chunk, way]).wait()
+            wait_all(gathered[way][chunk], 3, gather_send.at[chunk, way])
+    for way in range(2):
+        wait_all(codes_in.at[way], 3, codes_send.at[way])
     for step in range(STEPS):
         v = volume_ref if step == 0 else middle
         for k in range(4):
@@ -346,14 +456,21 @@
     return pltpu.VMEM(shape, jnp.float32)
 
 
-def solve(volume):
+def diffuse_and_route(volume, owners):
     dma = pltpu.SemaphoreType.DMA
     return pl.pallas_call(
-        solver_kernel,
-        out_shape=jax.ShapeDtypeStruct((ROWS, NX), jnp.float32),
-        in_specs=[pl.BlockSpec(memory_space=pltpu.VMEM)],
-        out_specs=pl.BlockSpec(memory_space=pltpu.VMEM),
+        diffuse_and_route_kernel,
+        out_shape=(
+            jax.ShapeDtypeStruct((ROWS, NX), jnp.float32),
+            jax.ShapeDtypeStruct((4, 4, MOST, BLOCK_ROWS, NX), jnp.float32),
+        ),
+        in_specs=[
+            pl.BlockSpec(memory_space=pl.ANY),
+            pl.BlockSpec(memory_space=pltpu.SMEM),
+        ],
+        out_specs=(pl.BlockSpec(memory_space=pltpu.VMEM), pl.BlockSpec(memory_space=pl.ANY)),
         scratch_shapes=[
+            vmem(ROWS, NX),
             vmem(ROWS, NX),
             vmem(STEPS, 2, CY, NX),
             vmem(STEPS, 2, CZ, NX),
@@ -374,30 +491,29 @@
             dma((STEPS, 4)),
             dma((STEPS, 4)),
         ]
-        + [dma((STEPS,))] * 8,
+        + [dma((STEPS,))] * 8
+        + [
+            pltpu.VMEM((8, NX), jnp.int32),
+            pltpu.VMEM((2, 4, 8, NX), jnp.int32),
+            pltpu.SMEM((2, 4, 8, NX), jnp.int32),
+            [[vmem(4, BLOCKS_HERE, CHUNK_ROWS, NX) for _ in range(CHUNKS)] for _ in range(2)],
+            vmem(2, 4, 4, MOST, HALF_ROWS, NX),
+            dma,
+            dma((2,)),
+            dma((2,)),
+            dma,
+        ]
+        + [dma((CHUNKS, 2))] * 5,
         compiler_params=pltpu.CompilerParams(
-            collective_id=0, has_side_effects=True, vmem_limit_bytes=32 << 20
+            collective_id=0, has_side_effects=True, vmem_limit_bytes=40 << 20
         ),
-    )(volume)
+    )(volume, owners)
 
 
 def on_device(volume, owners):
     depth, height, width = volume.shape
-    z_count = lax.axis_size("gz")
-    field = solve(volume.reshape(depth * height, width))
-    blocks = field.reshape(-1, BLOCK_ROWS, width)
-    targets = owners.reshape(-1)
-    block_count = targets.shape[0]
-    same = targets[:, None] == targets[None, :]
-    block_iota = jnp.arange(block_count, dtype=jnp.int32)
-    earlier = block_iota[:, None] < block_iota[None, :]
-    order_rank = jnp.sum((same & earlier).astype(jnp.int32), axis=0)
-    slot_index = targets * MOST + order_rank
-    outgoing = (
-        jnp.zeros((z_count * MOST, BLOCK_ROWS, width), field.dtype).at[slot_index].set(blocks)
-    )
-    incoming = lax.all_to_all(outgoing, "gz", split_axis=0, concat_axis=0, tiled=True)
-    return (field.reshape(volume.shape), incoming.reshape(1, z_count * MOST, BLOCK_ROWS, width))
+    field, routed = diffuse_and_route(volume.reshape(depth * height, width), owners.reshape(-1))
+    return (field.reshape(volume.shape), routed.reshape(1, N_GZ * MOST, BLOCK_ROWS, width))
 
 
 def solution(mesh):

time: 85.6 us -> 64.5 us (0.75)
  waiting for transfers between devices: 30.8 us -> 0 us
  Pallas kernels: 40.6 us -> 60 us
  starting transfers between devices: 5.02 us -> 0 us
  local copies, waits for them, and re-layouts: 6.72 us -> 3.62 us
  other arithmetic: 1.47 us -> 0 us
    all_to_all x1 -> x0, waiting for transfers between devices: 30.8 us -> none  [on_device(): lax.all_to_all(outgoing, 'gz', split_axis=0, concat_axis=0, tiled=True)]
    pallas_call x1, Pallas kernels: 40.6 us -> 60 us  [diffuse_and_route(): pl.pallas_call(diffuse_and_route_kernel, out_shape=(jax.ShapeDtypeStruct(...]
    all_to_all x1 -> x0, starting transfers between devices: 5.02 us -> none  [on_device(): lax.all_to_all(outgoing, 'gz', split_axis=0, concat_axis=0, tiled=True)]
    scatter x1 -> x0, local copies, waits for them, and re-layouts: 2.2 us -> none  [on_device(): jnp.zeros((z_count * MOST, BLOCK_ROWS, width), field.dtype).at[slot_index]]
    broadcast_in_dim x1 -> x0, local copies, waits for them, and re-layouts: 1.56 us -> none  [on_device(): jnp.zeros((z_count * MOST, BLOCK_ROWS, width), field.dtype).at[slot_index]]
    unnamed x4 -> x6, local copies, waits for them, and re-layouts: 2.96 us -> 3.62 us
  transfers between devices with their start and end apart: 1 -> 0, of which waited for: 1 -> 0; matrix products, arithmetic and copies ran while one was open for 0% -> 0% of each run, Pallas kernels for 0% -> 0%
where the time goes in v2:
time: 64.5 us; the launch traced here: 64.3 us
  Pallas kernels  60 us (93%)
  local copies, waits for them, and re-layouts  3.62 us (6%)
  between operations  0.65 us (1%)
    pallas_call x1, Pallas kernels, diffuse_and_route(): pl.pallas_call(diffuse_and_route_kernel, out_shape=(jax.ShapeDtypeStruct(...  60 us
    unnamed x6, local copies, waits for them, and re-layouts  3.62 us

profile of v2, /device:TPU:0, one launch (start us, length us, event | category | flops | bytes accessed | tf_op | source)
XLA Modules:
  0.0 64.3 jit_solution(8265811102630568951)
XLA Ops:
  0.6 0.0 copy-start
  0.6 0.9 %copy-done = f32[16,32,128]{2,1,0:T(8,128)S(1)} copy-done((f32[16,32,128]{2,1,0:T(8,128)S(1)}, f32[16,32,128]{2,1,0:T(8,128)}, u32[]{:S(2)}) %copy-start) | copy-done | bytes 262168
  1.6 0.0 copy-start.1
  1.6 0.7 %copy-done.1 = s32[1,4,1]{1,2,0:T(1,128)S(1)} copy-done((s32[1,4,1]{1,2,0:T(1,128)S(1)}, s32[1,4,1]{1,2,0:T(1,128)}, u32[]{:S(2)}) %copy-start.1) | copy-done | bytes 40
  2.2 60.0 %shard_map.41 = (f32[512,128]{1,0:T(8,128)S(1)}, f32[4,4,2,128,128]{4,3,2,1,0:T(8,128)S(1)}) custom-call(f32[512,128]{1,0:T(8,128)S(1)} %bitcast.5, s32[4]{0:T(128)S(1)} %bitcast.7), custom_call_target="tpu_custom_call" | custom-call | tf_op jit(solution)/shard_map/pallas_call | solution.py:461
  62.3 0.7 %copy.6 = f32[16,32,128]{2,1,0:T(8,128)} copy(f32[16,32,128]{2,1,0:T(8,128)S(1)} %bitcast.6) | data formatting | bytes 524288
  63.0 1.3 %copy.7 = f32[1,32,128,128]{3,2,1,0:T(8,128)} copy(f32[1,32,128,128]{3,2,1,0:T(8,128)S(1)} %bitcast.4) | data formatting | bytes 4194304
Async XLA Ops:
  0.6 1.0 %copy-start = (f32[16,32,128]{2,1,0:T(8,128)S(1)}, f32[16,32,128]{2,1,0:T(8,128)}, u32[]{:S(2)}) copy-start(f32[16,32,128]{2,1,0:T(8,128)} %param.2) | copy-start | bytes 786436
  1.6 0.7 %copy-start.1 = (s32[1,4,1]{1,2,0:T(1,128)S(1)}, s32[1,4,1]{1,2,0:T(1,128)}, u32[]{:S(2)}) copy-start(s32[1,4,1]{1,2,0:T(1,128)} %param.3) | copy-start | bytes 52

commit v3 on v2

--- a/solution.py
+++ b/solution.py
@@ -122,7 +122,7 @@
 
 def diffuse_and_route_kernel(
     volume_hbm,
-    owners_ref,
+    owners_hbm,
     out_ref,
     routed_ref,
     volume_ref,
@@ -153,6 +153,8 @@
     zb_recv,
     yb_send,
     yb_recv,
+    owners_ref,
+    owners_sem,
     codes_out,
     codes_in,
     codes,
@@ -170,6 +172,8 @@
 ):
     load_volume = pltpu.make_async_copy(volume_hbm, volume_ref, volume_sem)
     load_volume.start()
+    load_owners = pltpu.make_async_copy(owners_hbm, owners_ref, owners_sem)
+    load_owners.start()
     gz = lax.axis_index("gz")
     xy = lax.axis_index("xy")
     z_targets = [
@@ -193,7 +197,7 @@
             return chip_z * 4 + lax.rem(chip_y + offset, 4)
         return lax.rem(chip_z + offset, 4) * 4 + chip_y
 
-    own_codes = []
+    load_owners.wait()
     lanes = lax.broadcasted_iota(jnp.int32, (8, NX), 1)
     code_tile = jnp.zeros((8, NX), jnp.int32)
     for b in range(BLOCKS_HERE):
@@ -316,13 +320,13 @@
             base[rows, :] = pcr(diag, weight, v[rows, :], NX, 1)
             return carry
 
-        lax.fori_loop(0, CZ // 2, solve_x, 0)
+        lax.fori_loop(0, CZ // 4, solve_x, 0)
 
         def z_load(i):
             return z_keep[0, i], z_keep[1, i], z_keep[2, i]
 
         def z_restore(i, side, low, high):
-            base[i * CY : (i + 1) * CY, :] += side
+            natural[3, i * CY : (i + 1) * CY, :] = side
             z_keep[1, i] = low
             z_keep[2, i] = high
 
@@ -363,6 +367,7 @@
         send_all(yb_out, yb_in, yb_send.at[step], yb_recv.at[step], "xy", y_targets, xy)
         yb_in[xy] = yb_out[xy]
 
+        lax.fori_loop(CZ // 4, CZ // 2, solve_x, 0)
         wait_all(yb_in, N_XY - 1, yb_recv.at[step])
         wait_all(zb_in, N_GZ - 1, zb_recv.at[step])
         low_z = jnp.concatenate([z_back[step, pl.ds(h, N_GZ, stride=8), :] for h in (0, 1)], axis=0)
@@ -372,7 +377,7 @@
             at = (i % N_XY) * 8 + i // N_XY
             low_y = y_back[step, at : at + 1, :]
             high_y = y_back[step, at + 2 : at + 3, :]
-            total = base[rows, :] + natural[0, rows, :]
+            total = base[rows, :] + natural[0, rows, :] + natural[3, rows, :]
             total = total + (low_z * z_keep[1, i] - high_z * z_keep[2, i])
             total = total + (low_y * natural[1, rows, :] - high_y * natural[2, rows, :])
             new[rows, :] = total * (1.0 / 3.0)
@@ -465,8 +470,8 @@
             jax.ShapeDtypeStruct((4, 4, MOST, BLOCK_ROWS, NX), jnp.float32),
         ),
         in_specs=[
-            pl.BlockSpec(memory_space=pl.ANY),
-            pl.BlockSpec(memory_space=pltpu.SMEM),
+            pl.BlockSpec(memory_space=pltpu.HBM),
+            pl.BlockSpec(memory_space=pltpu.HBM),
         ],
         out_specs=(pl.BlockSpec(memory_space=pltpu.VMEM), pl.BlockSpec(memory_space=pl.ANY)),
         scratch_shapes=[
@@ -478,7 +483,7 @@
             vmem(ROWS, NX),
             vmem(3, CZ, CY, NX),
             vmem(3, CY, CZ, NX),
-            vmem(3, ROWS, NX),
+            vmem(4, ROWS, NX),
             vmem(ROWS, NX),
             vmem(STEPS, N_GZ * 16, NX),
             vmem(STEPS, N_GZ * 16, NX),
@@ -493,6 +498,8 @@
         ]
         + [dma((STEPS,))] * 8
         + [
+            pltpu.SMEM((BLOCKS_HERE,), jnp.int32),
+            dma,
             pltpu.VMEM((8, NX), jnp.int32),
             pltpu.VMEM((2, 4, 8, NX), jnp.int32),
             pltpu.SMEM((2, 4, 8, NX), jnp.int32),
@@ -505,7 +512,7 @@
         ]
         + [dma((CHUNKS, 2))] * 5,
         compiler_params=pltpu.CompilerParams(
-            collective_id=0, has_side_effects=True, vmem_limit_bytes=40 << 20
+            collective_id=0, has_side_effects=True, vmem_limit_bytes=48 << 20
         ),
     )(volume, owners)
 

time: 64.5 us -> 60.8 us (0.943); the launches traced: 64.3 us -> 59.7 us
  Pallas kernels: 60 us -> 55.4 us
    pallas_call x1, Pallas kernels: 60 us -> 55.4 us  [diffuse_and_route(): pl.pallas_call(diffuse_and_route_kernel, out_shape=(jax.ShapeDtypeStruct(...]
where the time goes in v3:
time: 60.8 us; the launch traced here: 59.7 us
  Pallas kernels  55.4 us (91%)
  local copies, waits for them, and re-layouts  3.62 us (6%)
  between operations  0.65 us (1%)
    pallas_call x1, Pallas kernels, diffuse_and_route(): pl.pallas_call(diffuse_and_route_kernel, out_shape=(jax.ShapeDtypeStruct(...  55.4 us
    unnamed x6, local copies, waits for them, and re-layouts  3.62 us

profile of v3, /device:TPU:0, one launch (start us, length us, event | category | flops | bytes accessed | tf_op | source)
XLA Modules:
  0.0 59.7 jit_solution(7831236884265102110)
XLA Ops:
  0.6 0.0 copy-start
  0.6 0.9 %copy-done = f32[16,32,128]{2,1,0:T(8,128)S(1)} copy-done((f32[16,32,128]{2,1,0:T(8,128)S(1)}, f32[16,32,128]{2,1,0:T(8,128)}, u32[]{:S(2)}) %copy-start) | copy-done | bytes 262168
  1.6 0.0 copy-start.1
  1.6 0.7 %copy-done.1 = s32[1,4,1]{1,2,0:T(1,128)S(1)} copy-done((s32[1,4,1]{1,2,0:T(1,128)S(1)}, s32[1,4,1]{1,2,0:T(1,128)}, u32[]{:S(2)}) %copy-start.1) | copy-done | bytes 40
  2.2 55.4 %shard_map.41 = (f32[512,128]{1,0:T(8,128)S(1)}, f32[4,4,2,128,128]{4,3,2,1,0:T(8,128)S(1)}) custom-call(f32[512,128]{1,0:T(8,128)S(1)} %bitcast.5, s32[4]{0:T(128)S(1)} %bitcast.7), custom_call_target="tpu_custom_call" | custom-call | tf_op jit(solution)/shard_map/pallas_call | solution.py:466
  57.7 0.7 %copy.6 = f32[16,32,128]{2,1,0:T(8,128)} copy(f32[16,32,128]{2,1,0:T(8,128)S(1)} %bitcast.6) | data formatting | bytes 524288
  58.4 1.3 %copy.7 = f32[1,32,128,128]{3,2,1,0:T(8,128)} copy(f32[1,32,128,128]{3,2,1,0:T(8,128)S(1)} %bitcast.4) | data formatting | bytes 4194304
Async XLA Ops:
  0.6 1.0 %copy-start = (f32[16,32,128]{2,1,0:T(8,128)S(1)}, f32[16,32,128]{2,1,0:T(8,128)}, u32[]{:S(2)}) copy-start(f32[16,32,128]{2,1,0:T(8,128)} %param.2) | copy-start | bytes 786436
  1.6 0.7 %copy-start.1 = (s32[1,4,1]{1,2,0:T(1,128)S(1)}, s32[1,4,1]{1,2,0:T(1,128)}, u32[]{:S(2)}) copy-start(s32[1,4,1]{1,2,0:T(1,128)} %param.3) | copy-start | bytes 52

commit v4 on v3

--- a/solution.py
+++ b/solution.py
@@ -20,9 +20,13 @@
 N_GZ = 16
 N_XY = 8
 FIELDS = 7
+Z_OWNERS = 8
+Y_OWNERS = 4
+LINES = 4
 BLOCKS_HERE = 4
 HALF_ROWS = BLOCK_ROWS // 2
 CHUNKS = 2
+X_FIRST = 4
 CHUNK_ROWS = HALF_ROWS // CHUNKS
 MESH = pl.DeviceIdType.MESH
 
@@ -104,7 +108,7 @@
         store(i, side, low_unit, high_unit)
 
 
-def interface_fluxes(received, count, half):
+def interface_fluxes(received, count):
     first_side, last_side, first_unit, cross, last_unit, g_first, g_last = [received(j) for j in range(FIELDS)]
     index = lax.broadcasted_iota(jnp.int32, (count, NX), 0)
 
@@ -182,6 +186,16 @@
     y_targets = [
         lax.rem(xy // 2 + dx, 4) * 2 + lax.rem(lax.rem(xy, 2) + core, 2) for dx, core in Y_PEERS
     ]
+    odd = lax.rem(gz + xy, 2)
+    joins_z = odd == 0
+    joins_y = odd == 1
+    z_owners = [
+        (lax.rem(gz // 4 + dz, 4) * 4 + lax.rem(lax.rem(gz, 4) + dy + odd, 4), (dz, dy) == (0, 0))
+        for dz, dy in ((2, 2), (1, 2), (3, 2), (2, 0), (1, 0), (3, 0), (0, 2), (0, 0))
+    ]
+    y_owners = [
+        (lax.rem(xy // 2 + dx, 4) * 2 + lax.rem(lax.rem(xy, 2) + 1 - odd, 2), dx == 0) for dx in (2, 1, 3, 0)
+    ]
     barrier = pltpu.get_barrier_semaphore()
     for target in z_targets:
         pl.semaphore_signal(barrier, 1, device_id={"gz": target}, device_id_type=MESH)
@@ -224,6 +238,31 @@
                 source.at[target], landing.at[me], send_sem, recv_sem,
                 device_id={axis: target}, device_id_type=MESH,
             ).start()
+
+    def send_parts(source, landing, send_sem, recv_sem, axis, owners, me, is_owner):
+        for target, may_be_self in owners:
+            copy = pltpu.make_async_remote_copy(
+                source.at[target // 2], landing.at[me], send_sem, recv_sem,
+                device_id={axis: target}, device_id_type=MESH,
+            )
+            if may_be_self:
+                pl.when(jnp.logical_not(is_owner))(copy.start)
+
+                @pl.when(is_owner)
+                def _():
+                    landing[me] = source[target // 2]
+
+            else:
+                copy.start()
+
+    def wait_parts(buffer, count, semaphore, is_owner):
+        @pl.when(is_owner)
+        def _():
+            wait_all(buffer, count - 1, semaphore)
+
+        @pl.when(jnp.logical_not(is_owner))
+        def _():
+            wait_all(buffer, count, semaphore)
 
     def wait_all(buffer, count, semaphore):
         part = buffer.at[pl.ds(0, count)]
@@ -285,11 +324,11 @@
 
         ends = forward_sweep(CZ, plane, lambda i: g_ref[i * CY : (i + 1) * CY, :], z_store)
         for j, field in enumerate(ends):
-            for half in range(2):
-                z_out[step, pl.ds(2 * j + half, N_GZ, stride=16), :] = field[half * N_GZ : (half + 1) * N_GZ, :]
-        z_in_blocks = z_in.at[step].reshape(N_GZ, 16, NX)
-        z_out_blocks = z_out.at[step].reshape(N_GZ, 16, NX)
-        send_all(z_out_blocks, z_in_blocks, z_send.at[step], z_recv.at[step], "gz", z_targets, gz)
+            for h in range(LINES):
+                z_out[step, pl.ds(LINES * j + h, Z_OWNERS, stride=32), :] = field[h * Z_OWNERS : (h + 1) * Z_OWNERS, :]
+        z_in_blocks = z_in.at[step].reshape(N_GZ, 32, NX)
+        z_out_blocks = z_out.at[step].reshape(Z_OWNERS, 32, NX)
+        send_parts(z_out_blocks, z_in_blocks, z_send.at[step], z_recv.at[step], "gz", z_owners, gz, joins_z)
 
         def y_store(i, ratio, side, unit):
             y_keep[0, i] = ratio
@@ -303,13 +342,11 @@
             y_store,
         )
         for j, field in enumerate(ends):
-            for half in range(2):
-                y_out[step, pl.ds(2 * j + half, N_XY, stride=16), :] = field[half * N_XY : (half + 1) * N_XY, :]
-        y_in_blocks = y_in.at[step].reshape(N_XY, 16, NX)
-        y_out_blocks = y_out.at[step].reshape(N_XY, 16, NX)
-        send_all(y_out_blocks, y_in_blocks, y_send.at[step], y_recv.at[step], "xy", y_targets, xy)
-        z_in_blocks[gz] = z_out_blocks[gz]
-        y_in_blocks[xy] = y_out_blocks[xy]
+            for h in range(LINES):
+                y_out[step, pl.ds(LINES * j + h, Y_OWNERS, stride=32), :] = field[h * Y_OWNERS : (h + 1) * Y_OWNERS, :]
+        y_in_blocks = y_in.at[step].reshape(N_XY, 32, NX)
+        y_out_blocks = y_out.at[step].reshape(Y_OWNERS, 32, NX)
+        send_parts(y_out_blocks, y_in_blocks, y_send.at[step], y_recv.at[step], "xy", y_owners, xy, joins_y)
 
         def solve_x(i, carry):
             rows = pl.ds(pl.multiple_of(i * 2 * CY, 2 * CY), 2 * CY)
@@ -320,7 +357,7 @@
             base[rows, :] = pcr(diag, weight, v[rows, :], NX, 1)
             return carry
 
-        lax.fori_loop(0, CZ // 4, solve_x, 0)
+        lax.fori_loop(0, X_FIRST, solve_x, 0)
 
         def z_load(i):
             return z_keep[0, i], z_keep[1, i], z_keep[2, i]
@@ -343,40 +380,47 @@
 
         backward_sweep(CY, y_load, y_restore)
 
-        wait_all(z_in_blocks, N_GZ - 1, z_recv.at[step])
         zb_out = z_back_out.at[step].reshape(N_GZ, 8, NX)
-        zb_in = z_back.at[step].reshape(N_GZ, 8, NX)
-        for half in range(2):
-            flux = interface_fluxes(
-                lambda j: z_in[step, pl.ds(2 * j + half, N_GZ, stride=16), :], N_GZ, half
-            )
-            z_back_out[step, pl.ds(half, N_GZ, stride=8), :] = pltpu.roll(flux, 1, 0)
-            z_back_out[step, pl.ds(2 + half, N_GZ, stride=8), :] = flux
-        send_all(zb_out, zb_in, zb_send.at[step], zb_recv.at[step], "gz", z_targets, gz)
-        zb_in[gz] = zb_out[gz]
-
-        wait_all(y_in_blocks, N_XY - 1, y_recv.at[step])
+        zb_in = z_back.at[step].reshape(Z_OWNERS, 8, NX)
         yb_out = y_back_out.at[step].reshape(N_XY, 8, NX)
-        yb_in = y_back.at[step].reshape(N_XY, 8, NX)
-        for half in range(2):
-            flux = interface_fluxes(
-                lambda j: y_in[step, pl.ds(2 * j + half, N_XY, stride=16), :], N_XY, half
-            )
-            y_back_out[step, pl.ds(half, N_XY, stride=8), :] = pltpu.roll(flux, 1, 0)
-            y_back_out[step, pl.ds(2 + half, N_XY, stride=8), :] = flux
-        send_all(yb_out, yb_in, yb_send.at[step], yb_recv.at[step], "xy", y_targets, xy)
-        yb_in[xy] = yb_out[xy]
-
-        lax.fori_loop(CZ // 4, CZ // 2, solve_x, 0)
-        wait_all(yb_in, N_XY - 1, yb_recv.at[step])
-        wait_all(zb_in, N_GZ - 1, zb_recv.at[step])
-        low_z = jnp.concatenate([z_back[step, pl.ds(h, N_GZ, stride=8), :] for h in (0, 1)], axis=0)
-        high_z = jnp.concatenate([z_back[step, pl.ds(2 + h, N_GZ, stride=8), :] for h in (0, 1)], axis=0)
+        yb_in = y_back.at[step].reshape(Y_OWNERS, 8, NX)
+
+        @pl.when(joins_z)
+        def _():
+            wait_all(z_in_blocks, N_GZ - 1, z_recv.at[step])
+            for h in range(LINES):
+                flux = interface_fluxes(
+                    lambda j: z_in[step, pl.ds(LINES * j + h, N_GZ, stride=32), :], N_GZ
+                )
+                z_back_out[step, pl.ds(h, N_GZ, stride=8), :] = pltpu.roll(flux, 1, 0)
+                z_back_out[step, pl.ds(LINES + h, N_GZ, stride=8), :] = flux
+            send_all(zb_out, zb_in, zb_send.at[step], zb_recv.at[step], "gz", z_targets, gz // 2)
+            zb_in[gz // 2] = zb_out[gz]
+
+        @pl.when(joins_y)
+        def _():
+            wait_all(y_in_blocks, N_XY - 1, y_recv.at[step])
+            for h in range(LINES):
+                flux = interface_fluxes(
+                    lambda j: y_in[step, pl.ds(LINES * j + h, N_XY, stride=32), :], N_XY
+                )
+                y_back_out[step, pl.ds(h, N_XY, stride=8), :] = pltpu.roll(flux, 1, 0)
+                y_back_out[step, pl.ds(LINES + h, N_XY, stride=8), :] = flux
+            send_all(yb_out, yb_in, yb_send.at[step], yb_recv.at[step], "xy", y_targets, xy // 2)
+            yb_in[xy // 2] = yb_out[xy]
+
+        lax.fori_loop(X_FIRST, CZ // 2, solve_x, 0)
+        wait_parts(yb_in, Y_OWNERS, yb_recv.at[step], joins_y)
+        wait_parts(zb_in, Z_OWNERS, zb_recv.at[step], joins_z)
+        low_z = jnp.concatenate([z_back[step, pl.ds(h, Z_OWNERS, stride=8), :] for h in range(LINES)], axis=0)
+        high_z = jnp.concatenate(
+            [z_back[step, pl.ds(LINES + h, Z_OWNERS, stride=8), :] for h in range(LINES)], axis=0
+        )
         for i in range(CZ):
             rows = slice(i * CY, (i + 1) * CY)
-            at = (i % N_XY) * 8 + i // N_XY
+            at = (i % Y_OWNERS) * 8 + i // Y_OWNERS
             low_y = y_back[step, at : at + 1, :]
-            high_y = y_back[step, at + 2 : at + 3, :]
+            high_y = y_back[step, at + LINES : at + LINES + 1, :]
             total = base[rows, :] + natural[0, rows, :] + natural[3, rows, :]
             total = total + (low_z * z_keep[1, i] - high_z * z_keep[2, i])
             total = total + (low_y * natural[1, rows, :] - high_y * natural[2, rows, :])
@@ -451,10 +495,16 @@
         for k in range(4):
             part = v.at[pl.ds(0, CY)] if k < 2 else y_halo_out.at[step, 0]
             pltpu.make_async_copy(part, part, halo_send.at[step, k]).wait()
-        wait_all(z_out.at[step].reshape(N_GZ, 16, NX), N_GZ - 1, z_send.at[step])
-        wait_all(y_out.at[step].reshape(N_XY, 16, NX), N_XY - 1, y_send.at[step])
-        wait_all(z_back_out.at[step].reshape(N_GZ, 8, NX), N_GZ - 1, zb_send.at[step])
-        wait_all(y_back_out.at[step].reshape(N_XY, 8, NX), N_XY - 1, yb_send.at[step])
+        wait_parts(z_out.at[step].reshape(Z_OWNERS, 32, NX), Z_OWNERS, z_send.at[step], joins_z)
+        wait_parts(y_out.at[step].reshape(Y_OWNERS, 32, NX), Y_OWNERS, y_send.at[step], joins_y)
+
+        @pl.when(joins_z)
+        def _():
+            wait_all(z_back_out.at[step].reshape(N_GZ, 8, NX), N_GZ - 1, zb_send.at[step])
+
+        @pl.when(joins_y)
+        def _():
+            wait_all(y_back_out.at[step].reshape(N_XY, 8, NX), N_XY - 1, yb_send.at[step])
 
 
 def vmem(*shape):
@@ -485,14 +535,14 @@
             vmem(3, CY, CZ, NX),
             vmem(4, ROWS, NX),
             vmem(ROWS, NX),
-            vmem(STEPS, N_GZ * 16, NX),
-            vmem(STEPS, N_GZ * 16, NX),
-            vmem(STEPS, N_XY * 16, NX),
-            vmem(STEPS, N_XY * 16, NX),
+            vmem(STEPS, Z_OWNERS * 32, NX),
+            vmem(STEPS, N_GZ * 32, NX),
+            vmem(STEPS, Y_OWNERS * 32, NX),
+            vmem(STEPS, N_XY * 32, NX),
             vmem(STEPS, N_GZ * 8, NX),
-            vmem(STEPS, N_GZ * 8, NX),
+            vmem(STEPS, Z_OWNERS * 8, NX),
             vmem(STEPS, N_XY * 8, NX),
-            vmem(STEPS, N_XY * 8, NX),
+            vmem(STEPS, Y_OWNERS * 8, NX),
             dma((STEPS, 4)),
             dma((STEPS, 4)),
         ]

time: 60.8 us -> 57.9 us (0.952); the launches traced: 59.7 us -> 57.7 us
  Pallas kernels: 55.4 us -> 53.5 us
    pallas_call x1, Pallas kernels: 55.4 us -> 53.5 us  [diffuse_and_route(): pl.pallas_call(diffuse_and_route_kernel, out_shape=(jax.ShapeDtypeStruct(...]
where the time goes in v4:
time: 57.9 us; the launch traced here: 57.7 us
  Pallas kernels  53.5 us (92%)
  local copies, waits for them, and re-layouts  3.62 us (6%)
  between operations  0.65 us (1%)
    pallas_call x1, Pallas kernels, diffuse_and_route(): pl.pallas_call(diffuse_and_route_kernel, out_shape=(jax.ShapeDtypeStruct(...  53.5 us
    unnamed x6, local copies, waits for them, and re-layouts  3.62 us

profile of v4, /device:TPU:0, one launch (start us, length us, event | category | flops | bytes accessed | tf_op | source)
XLA Modules:
  0.0 57.7 jit_solution(12689005332461409922)
XLA Ops:
  0.6 0.0 copy-start
  0.6 0.9 %copy-done = f32[16,32,128]{2,1,0:T(8,128)S(1)} copy-done((f32[16,32,128]{2,1,0:T(8,128)S(1)}, f32[16,32,128]{2,1,0:T(8,128)}, u32[]{:S(2)}) %copy-start) | copy-done | bytes 262168
  1.6 0.0 copy-start.1
  1.6 0.7 %copy-done.1 = s32[1,4,1]{1,2,0:T(1,128)S(1)} copy-done((s32[1,4,1]{1,2,0:T(1,128)S(1)}, s32[1,4,1]{1,2,0:T(1,128)}, u32[]{:S(2)}) %copy-start.1) | copy-done | bytes 40
  2.2 53.5 %shard_map.41 = (f32[512,128]{1,0:T(8,128)S(1)}, f32[4,4,2,128,128]{4,3,2,1,0:T(8,128)S(1)}) custom-call(f32[512,128]{1,0:T(8,128)S(1)} %bitcast.5, s32[4]{0:T(128)S(1)} %bitcast.7), custom_call_target="tpu_custom_call" | custom-call | tf_op jit(solution)/shard_map/pallas_call | solution.py:516
  55.7 0.7 %copy.6 = f32[16,32,128]{2,1,0:T(8,128)} copy(f32[16,32,128]{2,1,0:T(8,128)S(1)} %bitcast.6) | data formatting | bytes 524288
  56.4 1.3 %copy.7 = f32[1,32,128,128]{3,2,1,0:T(8,128)} copy(f32[1,32,128,128]{3,2,1,0:T(8,128)S(1)} %bitcast.4) | data formatting | bytes 4194304
Async XLA Ops:
  0.6 1.0 %copy-start = (f32[16,32,128]{2,1,0:T(8,128)S(1)}, f32[16,32,128]{2,1,0:T(8,128)}, u32[]{:S(2)}) copy-start(f32[16,32,128]{2,1,0:T(8,128)} %param.2) | copy-start | bytes 786436
  1.6 0.7 %copy-start.1 = (s32[1,4,1]{1,2,0:T(1,128)S(1)}, s32[1,4,1]{1,2,0:T(1,128)}, u32[]{:S(2)}) copy-start(s32[1,4,1]{1,2,0:T(1,128)} %param.3) | copy-start | bytes 52

commit v5 on v4

--- a/solution.py
+++ b/solution.py
@@ -564,12 +564,40 @@
         compiler_params=pltpu.CompilerParams(
             collective_id=0, has_side_effects=True, vmem_limit_bytes=48 << 20
         ),
-    )(volume, owners)
+    )(pltpu.with_memory_space_constraint(volume, pltpu.HBM), pltpu.with_memory_space_constraint(owners, pltpu.HBM))
+
+
+def write_kernel(field_ref, routed_ref, field_out, routed_out, semaphores):
+    copies = [pltpu.make_async_copy(field_ref, field_out, semaphores.at[0])]
+    for part in range(4):
+        rows = pl.ds(part * (N_GZ * MOST // 4), N_GZ * MOST // 4)
+        copies.append(
+            pltpu.make_async_copy(routed_ref.at[rows], routed_out.at[rows], semaphores.at[1 + part])
+        )
+    for copy in copies[::-1]:
+        copy.start()
+    for copy in copies:
+        copy.wait()
+
+
+def write_out(field, routed):
+    return pl.pallas_call(
+        write_kernel,
+        out_shape=(
+            jax.ShapeDtypeStruct(field.shape, field.dtype),
+            jax.ShapeDtypeStruct(routed.shape, routed.dtype),
+        ),
+        in_specs=[pl.BlockSpec(memory_space=pl.ANY)] * 2,
+        out_specs=(pl.BlockSpec(memory_space=pltpu.HBM),) * 2,
+        scratch_shapes=[pltpu.SemaphoreType.DMA((1 + 4,))],
+        compiler_params=pltpu.CompilerParams(vmem_limit_bytes=8 << 20),
+    )(field, routed)
 
 
 def on_device(volume, owners):
     depth, height, width = volume.shape
     field, routed = diffuse_and_route(volume.reshape(depth * height, width), owners.reshape(-1))
+    field, routed = write_out(field, routed.reshape(N_GZ * MOST, BLOCK_ROWS, width))
     return (field.reshape(volume.shape), routed.reshape(1, N_GZ * MOST, BLOCK_ROWS, width))
 
 

time: 57.9 us -> 55.7 us (0.962)
  local copies, waits for them, and re-layouts: 3.62 us -> 0 us
  Pallas kernels: 53.5 us -> 54.9 us
    unnamed x6 -> x0, local copies, waits for them, and re-layouts: 3.62 us -> none
    pallas_call x0 -> x1, Pallas kernels: none -> 1.45 us  [write_out(): pl.pallas_call(write_kernel, out_shape=(jax.ShapeDtypeStruct(field.shape,...]
where the time goes in v5:
time: 55.7 us; the launch traced here: 55.5 us
  Pallas kernels  54.9 us (99%)
  between operations  0.64 us (1%)
    pallas_call x1, Pallas kernels, diffuse_and_route(): pl.pallas_call(diffuse_and_route_kernel, out_shape=(jax.ShapeDtypeStruct(...  53.5 us
    pallas_call x1, Pallas kernels, write_out(): pl.pallas_call(write_kernel, out_shape=(jax.ShapeDtypeStruct(field.shape,...  1.45 us

profile of v5, /device:TPU:0, one launch (start us, length us, event | category | flops | bytes accessed | tf_op | source)
XLA Modules:
  0.0 55.5 jit_solution(15010951900133930281)
XLA Ops:
  0.6 53.5 %shard_map.41 = (f32[512,128]{1,0:T(8,128)S(1)}, f32[4,4,2,128,128]{4,3,2,1,0:T(8,128)S(1)}) custom-call(f32[512,128]{1,0:T(8,128)} %bitcast.6, s32[4]{0:T(128)} %bitcast.7), custom_call_target="tpu_custom_call" | custom-call | tf_op jit(solution)/shard_map/pallas_call | solution.py:516
  54.1 1.4 %shard_map.42 = (f32[512,128]{1,0:T(8,128)}, f32[32,128,128]{2,1,0:T(8,128)}) custom-call(f32[512,128]{1,0:T(8,128)S(1)} %get-tuple-element.6.field_ref, f32[32,128,128]{2,1,0:T(8,128)S(1)} %bitcast.5), custom_call_target="tpu_custom_call" | custom-call | tf_op jit(solution)/shard_map/pallas_call | solution.py:584

commit v6 on v5

--- a/solution.py
+++ b/solution.py
@@ -28,6 +28,7 @@
 CHUNKS = 2
 X_FIRST = 4
 CHUNK_ROWS = HALF_ROWS // CHUNKS
+PASSED_ROWS = CHUNK_ROWS // 2
 MESH = pl.DeviceIdType.MESH
 
 Z_PEERS = sorted(
@@ -162,15 +163,18 @@
     codes_out,
     codes_in,
     codes,
+    choice,
     gathered,
+    gathered_far,
     packed,
     volume_sem,
     codes_send,
     codes_recv,
     codes_sem,
-    own_sem,
     gather_send,
     gather_recv,
+    far_send,
+    far_recv,
     spread_send,
     spread_recv,
 ):
@@ -232,6 +236,56 @@
     row_index = lax.broadcasted_iota(jnp.int32, (CY, NX), 0)
     lane_index = lax.broadcasted_iota(jnp.int32, (CY, NX), 1)
 
+    blocks = out_ref.reshape(BLOCKS_HERE, BLOCK_ROWS, NX)
+    to_scalars = pltpu.make_async_copy(codes_in, codes, codes_sem)
+
+    def place_of(way, source):
+        return lax.rem(places[way] + (0, 3, 1, 2)[source], 4)
+
+    def choose():
+        for way in range(2):
+            for source in range(4):
+                place = place_of(way, source)
+                for offset in range(4):
+                    target = partner(1 - way, offset)
+                    for rank in range(MOST):
+                        index, found = 0, 0
+                        for b in range(BLOCKS_HERE):
+                            hit = (codes[way, place, 0, b] == target * MOST + rank).astype(jnp.int32)
+                            index = index + b * hit
+                            found = found + hit
+                        choice[0, way, source, offset, rank] = index
+                        choice[1, way, source, offset, rank] = found
+
+    def send_near(way, chunk):
+        here = pl.ds(way * HALF_ROWS + chunk * CHUNK_ROWS, CHUNK_ROWS)
+        for side, offset in ((0, 1), (1, 3)):
+            pltpu.make_async_remote_copy(
+                blocks.at[:, here, :], gathered[way][chunk].at[side],
+                gather_send.at[chunk, way], gather_recv.at[chunk, way],
+                device_id={"gz": partner(way, offset)}, device_id_type=MESH,
+            ).start()
+
+    def pass_on(way, source, offset, first, count, read):
+        there = pl.ds(first, count)
+        final = pl.ds(way * HALF_ROWS + first, count)
+        place = place_of(way, source)
+        at = (chip_z, place) if way == 0 else (place, chip_y)
+        for rank in range(MOST):
+            found = choice[1, way, source, offset, rank]
+            rows = jnp.where(found > 0, read(choice[0, way, source, offset, rank]), 0.0)
+            if offset:
+                packed[way, source, offset, rank, there, :] = rows
+            else:
+                routed_ref[at[0], at[1], rank, final, :] = rows
+        if offset:
+            kind = (0, 1, 1, 2)[source]
+            pltpu.make_async_remote_copy(
+                packed.at[way, source, offset, :, there, :], routed_ref.at[at[0], at[1], :, final, :],
+                spread_send.at[way, kind], spread_recv.at[way, kind],
+                device_id={"gz": partner(1 - way, offset)}, device_id_type=MESH,
+            ).start()
+
     def send_all(source, landing, send_sem, recv_sem, axis, targets, me):
         for target in targets:
             pltpu.make_async_remote_copy(
@@ -268,16 +322,13 @@
         part = buffer.at[pl.ds(0, count)]
         pltpu.make_async_copy(part, part, semaphore).wait()
 
-    for step in range(STEPS):
-        v = volume_ref if step == 0 else middle
-        new = out_ref if step == STEPS - 1 else middle
-
-        y_halo_out[step, 0] = v[pl.ds(0, CZ, stride=CY), :]
-        y_halo_out[step, 1] = v[pl.ds(CY - 1, CZ, stride=CY), :]
+    def halo_copies(step, v, which):
         copies = []
         for k, (axis, me, count, forward) in enumerate(
             [("gz", gz, N_GZ, 0), ("gz", gz, N_GZ, 1), ("xy", xy, N_XY, 0), ("xy", xy, N_XY, 1)]
         ):
+            if axis != which:
+                continue
             target = lax.rem(me + (1 if forward else count - 1), count)
             if axis == "gz":
                 source = v.at[pl.ds((CZ - 1) * CY if forward else 0, CY)]
@@ -291,19 +342,29 @@
                     device_id={axis: target}, device_id_type=MESH,
                 )
             )
-        for copy in copies:
+        return copies
+
+    def send_z_halo(step, v):
+        for copy in halo_copies(step, v, "gz"):
             copy.start()
-        for copy in copies:
-            copy.wait_recv()
+
+    def send_y_halo(step, v):
+        y_halo_out[step, 0] = v[pl.ds(0, CZ, stride=CY), :]
+        y_halo_out[step, 1] = v[pl.ds(CY - 1, CZ, stride=CY), :]
+        for copy in halo_copies(step, v, "xy"):
+            copy.start()
+
+    send_z_halo(0, volume_ref)
+    send_y_halo(0, volume_ref)
+    for step in range(STEPS):
+        v = volume_ref if step == 0 else middle
+        new = out_ref if step == STEPS - 1 else middle
 
         def plane(i):
             return v[i * CY : (i + 1) * CY, :]
 
-        before = jnp.where(gz == 0, plane(0), z_halo[step, 0])
-        after = jnp.where(gz == N_GZ - 1, plane(CZ - 1), z_halo[step, 1])
-        here = plane(0)
-        for i in range(CZ):
-            above = plane(i + 1) if i < CZ - 1 else after
+        def diffuse(i, before, above):
+            here = plane(i)
             slope_z = above - before
             y_low = jnp.where(xy == 0, here[0:1, :], y_halo[step, 0, i : i + 1, :])
             y_high = jnp.where(xy == N_XY - 1, here[CY - 1 : CY, :], y_halo[step, 1, i : i + 1, :])
@@ -315,7 +376,15 @@
             slope_x = x_next - x_prev
             squares = slope_z * slope_z + slope_y * slope_y + slope_x * slope_x
             g_ref[i * CY : (i + 1) * CY, :] = recip(1.0 + squares * (0.25 / CONTRAST))
-            before, here = here, above
+
+        for copy in halo_copies(step, v, "xy"):
+            copy.wait_recv()
+        for i in range(1, CZ - 1):
+            diffuse(i, plane(i - 1), plane(i + 1))
+        for copy in halo_copies(step, v, "gz"):
+            copy.wait_recv()
+        diffuse(0, jnp.where(gz == 0, plane(0), z_halo[step, 0]), plane(1))
+        diffuse(CZ - 1, plane(CZ - 2), jnp.where(gz == N_GZ - 1, plane(CZ - 1), z_halo[step, 1]))
 
         def z_store(i, ratio, side, unit):
             z_keep[0, i] = ratio
@@ -410,13 +479,17 @@
             yb_in[xy // 2] = yb_out[xy]
 
         lax.fori_loop(X_FIRST, CZ // 2, solve_x, 0)
+        if step == STEPS - 1:
+            to_scalars.wait()
+            choose()
         wait_parts(yb_in, Y_OWNERS, yb_recv.at[step], joins_y)
         wait_parts(zb_in, Z_OWNERS, zb_recv.at[step], joins_z)
         low_z = jnp.concatenate([z_back[step, pl.ds(h, Z_OWNERS, stride=8), :] for h in range(LINES)], axis=0)
         high_z = jnp.concatenate(
             [z_back[step, pl.ds(LINES + h, Z_OWNERS, stride=8), :] for h in range(LINES)], axis=0
         )
-        for i in range(CZ):
+
+        def combine(i):
             rows = slice(i * CY, (i + 1) * CY)
             at = (i % Y_OWNERS) * 8 + i // Y_OWNERS
             low_y = y_back[step, at : at + 1, :]
@@ -426,69 +499,65 @@
             total = total + (low_y * natural[1, rows, :] - high_y * natural[2, rows, :])
             new[rows, :] = total * (1.0 / 3.0)
 
-    for way in range(2):
-        wait_all(codes_in.at[way], 3, codes_recv.at[way])
-    to_scalars = pltpu.make_async_copy(codes_in, codes, codes_sem)
-    to_scalars.start()
-    blocks = out_ref.reshape(BLOCKS_HERE, BLOCK_ROWS, NX)
+        if step < STEPS - 1:
+            combine(0)
+            combine(CZ - 1)
+            send_z_halo(step + 1, new)
+            for i in range(1, CZ - 1):
+                combine(i)
+            send_y_halo(step + 1, new)
+            for way in range(2):
+                wait_all(codes_in.at[way], 3, codes_recv.at[way])
+            to_scalars.start()
+        else:
+            for chunk in range(CHUNKS):
+                for way in range(2):
+                    for b in range(BLOCKS_HERE):
+                        combine(b * 4 + way * 2 + chunk)
+                    send_near(way, chunk)
+
+    for offset in (1, 3, 2, 0):
+        for way in range(2):
+            here = pl.ds(way * HALF_ROWS, HALF_ROWS)
+            pass_on(way, 0, offset, 0, HALF_ROWS, lambda index: blocks[index, here, :])
     for chunk in range(CHUNKS):
         for way in range(2):
-            here = pl.ds(way * HALF_ROWS + chunk * CHUNK_ROWS, CHUNK_ROWS)
-            for offset in (2, 1, 3):
+            near = gathered[way][chunk]
+            wait_all(near, 2, gather_recv.at[chunk, way])
+            for side, offset in ((0, 1), (1, 3)):
+                rows = pl.ds(side * PASSED_ROWS, PASSED_ROWS)
+                landing = pl.ds(chunk * CHUNK_ROWS + side * PASSED_ROWS, PASSED_ROWS)
                 pltpu.make_async_remote_copy(
-                    blocks.at[:, here, :], gathered[way][chunk].at[places[way]],
-                    gather_send.at[chunk, way], gather_recv.at[chunk, way],
+                    near.at[side, :, rows, :], gathered_far[way].at[:, landing, :],
+                    far_send.at[way], far_recv.at[way],
                     device_id={"gz": partner(way, offset)}, device_id_type=MESH,
                 ).start()
+    for chunk in range(CHUNKS):
+        for offset in (1, 3, 2, 0):
+            for side in range(2):
+                for way in range(2):
+                    near = gathered[way][chunk]
+                    pass_on(
+                        way, 1 + side, offset, chunk * CHUNK_ROWS, CHUNK_ROWS, lambda index: near[side, index]
+                    )
     for way in range(2):
+        wait_all(gathered_far[way], BLOCKS_HERE, far_recv.at[way])
+    for offset in (1, 3, 2, 0):
+        for way in range(2):
+            pass_on(way, 3, offset, 0, HALF_ROWS, lambda index: gathered_far[way][index])
+    for way in range(2):
+        for kind, part in enumerate(
+            (
+                packed.at[way, 0, pl.ds(0, 3)],
+                packed.at[way, pl.ds(1, 2), pl.ds(0, 3)],
+                packed.at[way, 3, pl.ds(0, 3)],
+            )
+        ):
+            pltpu.make_async_copy(part, part, spread_recv.at[way, kind]).wait()
+            pltpu.make_async_copy(part, part, spread_send.at[way, kind]).wait()
         for chunk in range(CHUNKS):
-            here = pl.ds(way * HALF_ROWS + chunk * CHUNK_ROWS, CHUNK_ROWS)
-            gathered[way][chunk][places[way]] = blocks[:, here, :]
-    to_scalars.wait()
-    choice = {}
-    for way in range(2):
-        for offset in range(4):
-            target = partner(1 - way, offset)
-            for source in range(4):
-                for rank in range(MOST):
-                    index, found = 0, 0
-                    for b in range(BLOCKS_HERE):
-                        hit = (codes[way, source, 0, b] == target * MOST + rank).astype(jnp.int32)
-                        index = index + b * hit
-                        found = found + hit
-                    choice[way, offset, source, rank] = index, found
-    for chunk in range(CHUNKS):
-        for way in range(2):
-            there = pl.ds(chunk * CHUNK_ROWS, CHUNK_ROWS)
-            final = pl.ds(way * HALF_ROWS + chunk * CHUNK_ROWS, CHUNK_ROWS)
-            wait_all(gathered[way][chunk], 3, gather_recv.at[chunk, way])
-            for offset in (2, 1, 3, 0):
-                for source in range(4):
-                    for rank in range(MOST):
-                        index, found = choice[way, offset, source, rank]
-                        rows = gathered[way][chunk][source, index]
-                        packed[way, offset, source, rank, there, :] = jnp.where(found > 0, rows, 0.0)
-                landing = routed_ref.at[chip_z, :, :, final, :] if way == 0 else routed_ref.at[:, chip_y, :, final, :]
-                if offset:
-                    pltpu.make_async_remote_copy(
-                        packed.at[way, offset, :, :, there, :], landing,
-                        spread_send.at[chunk, way], spread_recv.at[chunk, way],
-                        device_id={"gz": partner(1 - way, offset)}, device_id_type=MESH,
-                    ).start()
-                else:
-                    pltpu.make_async_copy(
-                        packed.at[way, offset, :, :, there, :], landing, own_sem.at[chunk, way]
-                    ).start()
-    for chunk in range(CHUNKS):
-        for way in range(2):
-            there = pl.ds(chunk * CHUNK_ROWS, CHUNK_ROWS)
-            part = packed.at[way, pl.ds(0, 3), :, :, there, :]
-            pltpu.make_async_copy(part, part, spread_recv.at[chunk, way]).wait()
-            pltpu.make_async_copy(part, part, spread_send.at[chunk, way]).wait()
-            part = packed.at[way, 0, :, :, there, :]
-            pltpu.make_async_copy(part, part, own_sem.at[chunk, way]).wait()
-            wait_all(gathered[way][chunk], 3, gather_send.at[chunk, way])
-    for way in range(2):
+            wait_all(gathered[way][chunk], 2, gather_send.at[chunk, way])
+        wait_all(gathered_far[way], BLOCKS_HERE, far_send.at[way])
         wait_all(codes_in.at[way], 3, codes_send.at[way])
     for step in range(STEPS):
         v = volume_ref if step == 0 else middle
@@ -523,7 +592,7 @@
             pl.BlockSpec(memory_space=pltpu.HBM),
             pl.BlockSpec(memory_space=pltpu.HBM),
         ],
-        out_specs=(pl.BlockSpec(memory_space=pltpu.VMEM), pl.BlockSpec(memory_space=pl.ANY)),
+        out_specs=(pl.BlockSpec(memory_space=pltpu.VMEM),) * 2,
         scratch_shapes=[
             vmem(ROWS, NX),
             vmem(ROWS, NX),
@@ -553,14 +622,18 @@
             pltpu.VMEM((8, NX), jnp.int32),
             pltpu.VMEM((2, 4, 8, NX), jnp.int32),
             pltpu.SMEM((2, 4, 8, NX), jnp.int32),
-            [[vmem(4, BLOCKS_HERE, CHUNK_ROWS, NX) for _ in range(CHUNKS)] for _ in range(2)],
+            pltpu.SMEM((2, 2, 4, 4, MOST), jnp.int32),
+            [[vmem(2, BLOCKS_HERE, CHUNK_ROWS, NX) for _ in range(CHUNKS)] for _ in range(2)],
+            [vmem(BLOCKS_HERE, HALF_ROWS, NX) for _ in range(2)],
             vmem(2, 4, 4, MOST, HALF_ROWS, NX),
             dma,
             dma((2,)),
             dma((2,)),
             dma,
         ]
-        + [dma((CHUNKS, 2))] * 5,
+        + [dma((CHUNKS, 2))] * 2
+        + [dma((2,))] * 2
+        + [dma((2, 3))] * 2,
         compiler_params=pltpu.CompilerParams(
             collective_id=0, has_side_effects=True, vmem_limit_bytes=48 << 20
         ),

time: 55.7 us -> 54.8 us (0.984)
  Pallas kernels: 54.9 us -> 54.1 us
    pallas_call x1, Pallas kernels: 53.5 us -> 52.6 us  [diffuse_and_route(): pl.pallas_call(diffuse_and_route_kernel, out_shape=(jax.ShapeDtypeStruct(...]
where the time goes in v6:
time: 54.8 us; the launch traced here: 54.7 us
  Pallas kernels  54.1 us (99%)
  between operations  0.64 us (1%)
    pallas_call x1, Pallas kernels, diffuse_and_route(): pl.pallas_call(diffuse_and_route_kernel, out_shape=(jax.ShapeDtypeStruct(...  52.6 us
    pallas_call x1, Pallas kernels, write_out(): pl.pallas_call(write_kernel, out_shape=(jax.ShapeDtypeStruct(field.shape,...  1.45 us

profile of v6, /device:TPU:0, one launch (start us, length us, event | category | flops | bytes accessed | tf_op | source)
XLA Modules:
  0.0 54.7 jit_solution(11680584015768870314)
XLA Ops:
  0.6 52.6 %shard_map.41 = (f32[512,128]{1,0:T(8,128)S(1)}, f32[4,4,2,128,128]{4,3,2,1,0:T(8,128)S(1)}) custom-call(f32[512,128]{1,0:T(8,128)} %bitcast.6, s32[4]{0:T(128)} %bitcast.7), custom_call_target="tpu_custom_call" | custom-call | tf_op jit(solution)/shard_map/pallas_call | solution.py:585
  53.3 1.4 %shard_map.42 = (f32[512,128]{1,0:T(8,128)}, f32[32,128,128]{2,1,0:T(8,128)}) custom-call(f32[512,128]{1,0:T(8,128)S(1)} %get-tuple-element.6.field_ref, f32[32,128,128]{2,1,0:T(8,128)S(1)} %bitcast.5), custom_call_target="tpu_custom_call" | custom-call | tf_op jit(solution)/shard_map/pallas_call | solution.py:657

commit v7 on v6

--- a/solution.py
+++ b/solution.py
@@ -26,7 +26,8 @@
 BLOCKS_HERE = 4
 HALF_ROWS = BLOCK_ROWS // 2
 CHUNKS = 2
-X_FIRST = 4
+X_ROWS = 4 * CY
+X_FIRST = 2
 CHUNK_ROWS = HALF_ROWS // CHUNKS
 PASSED_ROWS = CHUNK_ROWS // 2
 MESH = pl.DeviceIdType.MESH
@@ -178,10 +179,6 @@
     spread_send,
     spread_recv,
 ):
-    load_volume = pltpu.make_async_copy(volume_hbm, volume_ref, volume_sem)
-    load_volume.start()
-    load_owners = pltpu.make_async_copy(owners_hbm, owners_ref, owners_sem)
-    load_owners.start()
     gz = lax.axis_index("gz")
     xy = lax.axis_index("xy")
     z_targets = [
@@ -205,6 +202,10 @@
         pl.semaphore_signal(barrier, 1, device_id={"gz": target}, device_id_type=MESH)
     for target in y_targets:
         pl.semaphore_signal(barrier, 1, device_id={"xy": target}, device_id_type=MESH)
+    load_volume = pltpu.make_async_copy(volume_hbm, volume_ref, volume_sem)
+    load_volume.start()
+    load_owners = pltpu.make_async_copy(owners_hbm, owners_ref, owners_sem)
+    load_owners.start()
     pl.semaphore_wait(barrier, N_GZ + N_XY - 2)
 
     chip_z, chip_y = gz // 4, lax.rem(gz, 4)
@@ -215,22 +216,6 @@
             return chip_z * 4 + lax.rem(chip_y + offset, 4)
         return lax.rem(chip_z + offset, 4) * 4 + chip_y
 
-    load_owners.wait()
-    lanes = lax.broadcasted_iota(jnp.int32, (8, NX), 1)
-    code_tile = jnp.zeros((8, NX), jnp.int32)
-    for b in range(BLOCKS_HERE):
-        rank = 0
-        for earlier in range(b):
-            rank = rank + (owners_ref[earlier] == owners_ref[b]).astype(jnp.int32)
-        code_tile = jnp.where(lanes == b, owners_ref[b] * MOST + rank, code_tile)
-    codes_out[...] = code_tile
-    for way in range(2):
-        codes_in[way, places[way]] = code_tile
-        for offset in (2, 1, 3):
-            pltpu.make_async_remote_copy(
-                codes_out, codes_in.at[way, places[way]], codes_send.at[way], codes_recv.at[way],
-                device_id={"gz": partner(way, offset)}, device_id_type=MESH,
-            ).start()
     load_volume.wait()
 
     row_index = lax.broadcasted_iota(jnp.int32, (CY, NX), 0)
@@ -356,6 +341,22 @@
 
     send_z_halo(0, volume_ref)
     send_y_halo(0, volume_ref)
+    load_owners.wait()
+    lanes = lax.broadcasted_iota(jnp.int32, (8, NX), 1)
+    code_tile = jnp.zeros((8, NX), jnp.int32)
+    for b in range(BLOCKS_HERE):
+        rank = 0
+        for earlier in range(b):
+            rank = rank + (owners_ref[earlier] == owners_ref[b]).astype(jnp.int32)
+        code_tile = jnp.where(lanes == b, owners_ref[b] * MOST + rank, code_tile)
+    codes_out[...] = code_tile
+    for way in range(2):
+        codes_in[way, places[way]] = code_tile
+        for offset in (2, 1, 3):
+            pltpu.make_async_remote_copy(
+                codes_out, codes_in.at[way, places[way]], codes_send.at[way], codes_recv.at[way],
+                device_id={"gz": partner(way, offset)}, device_id_type=MESH,
+            ).start()
     for step in range(STEPS):
         v = volume_ref if step == 0 else middle
         new = out_ref if step == STEPS - 1 else middle
@@ -418,9 +419,9 @@
         send_parts(y_out_blocks, y_in_blocks, y_send.at[step], y_recv.at[step], "xy", y_owners, xy, joins_y)
 
         def solve_x(i, carry):
-            rows = pl.ds(pl.multiple_of(i * 2 * CY, 2 * CY), 2 * CY)
+            rows = pl.ds(pl.multiple_of(i * X_ROWS, X_ROWS), X_ROWS)
             g = g_ref[rows, :]
-            lanes = lax.broadcasted_iota(jnp.int32, (2 * CY, NX), 1)
+            lanes = lax.broadcasted_iota(jnp.int32, (X_ROWS, NX), 1)
             weight = jnp.where(lanes < NX - 1, HALF_K * (g + pltpu.roll(g, NX - 1, 1)), 0.0)
             diag = 1.0 + weight + pltpu.roll(weight, 1, 1)
             base[rows, :] = pcr(diag, weight, v[rows, :], NX, 1)
@@ -478,10 +479,7 @@
             send_all(yb_out, yb_in, yb_send.at[step], yb_recv.at[step], "xy", y_targets, xy // 2)
             yb_in[xy // 2] = yb_out[xy]
 
-        lax.fori_loop(X_FIRST, CZ // 2, solve_x, 0)
-        if step == STEPS - 1:
-            to_scalars.wait()
-            choose()
+        lax.fori_loop(X_FIRST, ROWS // X_ROWS, solve_x, 0)
         wait_parts(yb_in, Y_OWNERS, yb_recv.at[step], joins_y)
         wait_parts(zb_in, Z_OWNERS, zb_recv.at[step], joins_z)
         low_z = jnp.concatenate([z_back[step, pl.ds(h, Z_OWNERS, stride=8), :] for h in range(LINES)], axis=0)
@@ -509,6 +507,8 @@
             for way in range(2):
                 wait_all(codes_in.at[way], 3, codes_recv.at[way])
             to_scalars.start()
+            to_scalars.wait()
+            choose()
         else:
             for chunk in range(CHUNKS):
                 for way in range(2):

time: 54.8 us -> 54 us (0.985)
  Pallas kernels: 54.1 us -> 53.3 us
    pallas_call x1, Pallas kernels: 52.6 us -> 51.8 us  [diffuse_and_route(): pl.pallas_call(diffuse_and_route_kernel, out_shape=(jax.ShapeDtypeStruct(...]
where the time goes in v7:
time: 54 us; the launch traced here: 53.9 us
  Pallas kernels  53.3 us (99%)
  between operations  0.64 us (1%)
    pallas_call x1, Pallas kernels, diffuse_and_route(): pl.pallas_call(diffuse_and_route_kernel, out_shape=(jax.ShapeDtypeStruct(...  51.8 us
    pallas_call x1, Pallas kernels, write_out(): pl.pallas_call(write_kernel, out_shape=(jax.ShapeDtypeStruct(field.shape,...  1.45 us

profile of v7, /device:TPU:0, one launch (start us, length us, event | category | flops | bytes accessed | tf_op | source)
XLA Modules:
  0.0 53.9 jit_solution(15962918432221770482)
XLA Ops:
  0.6 51.8 %shard_map.41 = (f32[512,128]{1,0:T(8,128)S(1)}, f32[4,4,2,128,128]{4,3,2,1,0:T(8,128)S(1)}) custom-call(f32[512,128]{1,0:T(8,128)} %bitcast.6, s32[4]{0:T(128)} %bitcast.7), custom_call_target="tpu_custom_call" | custom-call | tf_op jit(solution)/shard_map/pallas_call | solution.py:585
  52.5 1.4 %shard_map.42 = (f32[512,128]{1,0:T(8,128)}, f32[32,128,128]{2,1,0:T(8,128)}) custom-call(f32[512,128]{1,0:T(8,128)S(1)} %get-tuple-element.6.field_ref, f32[32,128,128]{2,1,0:T(8,128)S(1)} %bitcast.5), custom_call_target="tpu_custom_call" | custom-call | tf_op jit(solution)/shard_map/pallas_call | solution.py:657

commit v8 on v7

--- a/solution.py
+++ b/solution.py
@@ -29,7 +29,6 @@
 X_ROWS = 4 * CY
 X_FIRST = 2
 CHUNK_ROWS = HALF_ROWS // CHUNKS
-PASSED_ROWS = CHUNK_ROWS // 2
 MESH = pl.DeviceIdType.MESH
 
 Z_PEERS = sorted(
@@ -524,26 +523,23 @@
         for way in range(2):
             near = gathered[way][chunk]
             wait_all(near, 2, gather_recv.at[chunk, way])
-            for side, offset in ((0, 1), (1, 3)):
-                rows = pl.ds(side * PASSED_ROWS, PASSED_ROWS)
-                landing = pl.ds(chunk * CHUNK_ROWS + side * PASSED_ROWS, PASSED_ROWS)
-                pltpu.make_async_remote_copy(
-                    near.at[side, :, rows, :], gathered_far[way].at[:, landing, :],
-                    far_send.at[way], far_recv.at[way],
-                    device_id={"gz": partner(way, offset)}, device_id_type=MESH,
-                ).start()
-    for chunk in range(CHUNKS):
-        for offset in (1, 3, 2, 0):
-            for side in range(2):
-                for way in range(2):
-                    near = gathered[way][chunk]
-                    pass_on(
-                        way, 1 + side, offset, chunk * CHUNK_ROWS, CHUNK_ROWS, lambda index: near[side, index]
-                    )
+            side, offset = ((0, 1), (1, 3))[chunk % 2]
+            landing = pl.ds(chunk * CHUNK_ROWS, CHUNK_ROWS)
+            pltpu.make_async_remote_copy(
+                near.at[side], gathered_far[way].at[:, landing, :],
+                far_send.at[way], far_recv.at[way],
+                device_id={"gz": partner(way, offset)}, device_id_type=MESH,
+            ).start()
+    for offset in (1, 3, 2, 0):
+        for side in range(2):
+            for way in range(2):
+                pass_on(
+                    way, 1 + side, offset, 0, HALF_ROWS,
+                    lambda index: jnp.concatenate([gathered[way][chunk][side, index] for chunk in range(CHUNKS)], axis=0),
+                )
     for way in range(2):
         wait_all(gathered_far[way], BLOCKS_HERE, far_recv.at[way])
-    for offset in (1, 3, 2, 0):
-        for way in range(2):
+        for offset in (1, 3, 2, 0):
             pass_on(way, 3, offset, 0, HALF_ROWS, lambda index: gathered_far[way][index])
     for way in range(2):
         for kind, part in enumerate(

time: 54 us -> 54 us (level)
  no operation moved by 1% of the time
where the time goes in v8:
time: 54 us; the launch traced here: 53.9 us
  Pallas kernels  53.3 us (99%)
  between operations  0.64 us (1%)
    pallas_call x1, Pallas kernels, diffuse_and_route(): pl.pallas_call(diffuse_and_route_kernel, out_shape=(jax.ShapeDtypeStruct(...  51.8 us
    pallas_call x1, Pallas kernels, write_out(): pl.pallas_call(write_kernel, out_shape=(jax.ShapeDtypeStruct(field.shape,...  1.45 us

profile of v8, /device:TPU:0, one launch (start us, length us, event | category | flops | bytes accessed | tf_op | source)
XLA Modules:
  0.0 53.9 jit_solution(1222094957617000014)
XLA Ops:
  0.6 51.8 %shard_map.41 = (f32[512,128]{1,0:T(8,128)S(1)}, f32[4,4,2,128,128]{4,3,2,1,0:T(8,128)S(1)}) custom-call(f32[512,128]{1,0:T(8,128)} %bitcast.6, s32[4]{0:T(128)} %bitcast.7), custom_call_target="tpu_custom_call" | custom-call | tf_op jit(solution)/shard_map/pallas_call | solution.py:581
  52.5 1.4 %shard_map.42 = (f32[512,128]{1,0:T(8,128)}, f32[32,128,128]{2,1,0:T(8,128)}) custom-call(f32[512,128]{1,0:T(8,128)S(1)} %get-tuple-element.6.field_ref, f32[32,128,128]{2,1,0:T(8,128)S(1)} %bitcast.5), custom_call_target="tpu_custom_call" | custom-call | tf_op jit(solution)/shard_map/pallas_call | solution.py:653

commit v9 on v8

--- a/solution.py
+++ b/solution.py
@@ -426,7 +426,7 @@
             base[rows, :] = pcr(diag, weight, v[rows, :], NX, 1)
             return carry
 
-        lax.fori_loop(0, X_FIRST, solve_x, 0)
+        lax.fori_loop(0, X_FIRST, solve_x, 0, unroll=True)
 
         def z_load(i):
             return z_keep[0, i], z_keep[1, i], z_keep[2, i]

time: 54 us -> 54 us (level)
  no operation moved by 1% of the time
where the time goes in v9:
time: 54 us; the launch traced here: 53.9 us
  Pallas kernels  53.3 us (99%)
  between operations  0.64 us (1%)
    pallas_call x1, Pallas kernels, diffuse_and_route(): pl.pallas_call(diffuse_and_route_kernel, out_shape=(jax.ShapeDtypeStruct(...  51.8 us
    pallas_call x1, Pallas kernels, write_out(): pl.pallas_call(write_kernel, out_shape=(jax.ShapeDtypeStruct(field.shape,...  1.45 us

profile of v9, /device:TPU:0, one launch (start us, length us, event | category | flops | bytes accessed | tf_op | source)
XLA Modules:
  0.0 53.9 jit_solution(3005206768876063409)
XLA Ops:
  0.6 51.8 %shard_map.41 = (f32[512,128]{1,0:T(8,128)S(1)}, f32[4,4,2,128,128]{4,3,2,1,0:T(8,128)S(1)}) custom-call(f32[512,128]{1,0:T(8,128)} %bitcast.6, s32[4]{0:T(128)} %bitcast.7), custom_call_target="tpu_custom_call" | custom-call | tf_op jit(solution)/shard_map/pallas_call | solution.py:581
  52.5 1.4 %shard_map.42 = (f32[512,128]{1,0:T(8,128)}, f32[32,128,128]{2,1,0:T(8,128)}) custom-call(f32[512,128]{1,0:T(8,128)S(1)} %get-tuple-element.6.field_ref, f32[32,128,128]{2,1,0:T(8,128)S(1)} %bitcast.5), custom_call_target="tpu_custom_call" | custom-call | tf_op jit(solution)/shard_map/pallas_call | solution.py:653
